TPU v7x, 32 devices: a whole 2x2x4 slice. The times are simulated.
32 devices in a mesh: expert: 8 (over z, y), tensor: 4 (over x, core).
Axes of the slice: x: 2, y: 2, z: 4, core: 2. Of those that a mesh axis runs over, the one named last changes fastest.
Arguments:
- inputs: bfloat16 [4096, 768], P(('expert', 'tensor')), may hold values from -6 to 6
- projection: bfloat16 [3, 768, 768], P(None, None, 'tensor'), may hold values from -0.21875 to 0.21875
- output_weight: bfloat16 [768, 768], P('tensor'), may hold values from -1.25 to 1.25
- first_gain: float32 [768], replicated, may hold values from 0.1 to 1.9
- second_gain: float32 [768], replicated, may hold values from 0.1 to 1.9
- bias_table: float32 [12, 32], P('tensor'), may hold values from -4 to 4
- bucket_map: int32 [512], replicated, may hold values from 0 to 31, as said below
- router_weight: bfloat16 [768, 8], replicated, may hold values from -0.15625 to 0.15625
- routing: int32 [4096, 2], P(('expert', 'tensor')), may hold values from 0 to 7, all different within a row; in each aligned block of 128 rows (0 to 127, 128 to 255, ...) at most 48 rows name the same one
- expert_up: bfloat16 [8, 768, 3072], P('expert', None, 'tensor'), may hold values from -0.21875 to 0.21875
- expert_down: bfloat16 [8, 3072, 768], P('expert', 'tensor'), may hold values from -0.109375 to 0.109375
- cotangent: bfloat16 [4096, 768], P(('expert', 'tensor')), may hold values from -6 to 6
Outputs:
- result: bfloat16 [4096, 768], P(('expert', 'tensor'))
- grad_inputs: float32 [4096, 768], P(('expert', 'tensor'))
- grad_projection: float32 [3, 768, 768], P(None, None, 'tensor')
- grad_output: float32 [768, 768], P('tensor')
- grad_first: float32 [768], replicated
- grad_second: float32 [768], replicated
- grad_table: float32 [12, 32], P('tensor')
- grad_router: float32 [768, 8], replicated
- grad_up: float32 [8, 768, 3072], P('expert', None, 'tensor')
- grad_down: float32 [8, 3072, 768], P('expert', 'tensor')
Inputs may be any that keep to these rules, and one draw needn't show every extreme that they name: `routing`: each row names 2 different experts. In the rows of one device (aligned blocks of 128 rows) no expert is named by more than 48 rows, and in some blocks one expert is named by exactly 48 rows. `bucket_map`: nondecreasing in the distance, 0 at distance 0; every one of the 32 buckets is used.
All inputs are finite; a program needn't handle non-finite values.
Results may differ from a plain program's by a relative error of at most 0.019.
Values may be sent and summed in bfloat16 or wider, within the bound.
A program may use at most 128 MiB of HBM per device.

v0:
```python
from functools import partial

import jax
import jax.numpy as jnp
from jax import lax
from jax.sharding import PartitionSpec as P

epsilon = 1e-06
negative = -1e30
highest = lax.Precision.HIGHEST


def normalize(values, scale_gain):
    return (
        values * lax.rsqrt(jnp.mean(values * values, axis=-1, keepdims=True) + epsilon) * scale_gain
    )


def block_bias(table_rows, bucket_hot, offset, height, length):
    per_distance = jnp.dot(table_rows, bucket_hot, precision=highest)
    reverse = jnp.concatenate([per_distance[:, ::-1], jnp.zeros_like(per_distance)], axis=1)
    tiled_rows = jnp.tile(reverse, (1, height + 1))
    start_at = length - 1 - offset
    window = tiled_rows[:, start_at : start_at + height * (2 * length - 1)]
    return window.reshape(table_rows.shape[0], height, 2 * length - 1)[:, :, :length]


def block_scores(query_block, key_rows, table_rows, bucket_hot, offset, length, scaling):
    height = query_block.shape[1]
    raw_scores = jnp.einsum(
        "hqd,hkd->hqk", query_block, key_rows, preferred_element_type=jnp.float32
    )
    scores = raw_scores * scaling + block_bias(table_rows, bucket_hot, offset, height, length)
    row_at = offset + jnp.arange(height, dtype=jnp.int32)[:, None]
    column_at = jnp.arange(length, dtype=jnp.int32)[None, :]
    return jnp.where((column_at <= row_at)[None], scores, negative)


def repeated(values, copies):
    return jnp.broadcast_to(values[None], (copies,) + values.shape)


def per_device(
    inputs,
    projection,
    output_weight,
    first_gain,
    second_gain,
    bias_table,
    bucket_map,
    router_weight,
    routing,
    expert_up,
    expert_down,
    cotangent,
):
    tensor_count = lax.axis_size("tensor")
    tensor_index = lax.axis_index("tensor")
    local_rows = inputs.shape[0]
    experts = router_weight.shape[1]
    route_count = routing.shape[1]
    local_experts = expert_up.shape[0]
    capacity = max(2, 3 * route_count * local_rows // (2 * experts))
    length = local_rows * tensor_count
    heads_here = bias_table.shape[0]
    width_here = projection.shape[2]
    head_size = width_here // heads_here
    scaling = head_size ** (-0.5)
    height = min(512, length)
    slot_count = experts * capacity
    assignments = local_rows * route_count

    def heads_first(matrix):
        return matrix.reshape(length, heads_here, head_size).transpose(1, 0, 2)

    def heads_last(tensor_value):
        return tensor_value.transpose(1, 0, 2).reshape(length, width_here)

    def split_experts(flat_rows):
        view = flat_rows.reshape(-1, local_experts, flat_rows.shape[-1])
        return [view[:, 0]]

    def join_experts(pieces):
        return jnp.stack(pieces, axis=1).reshape(-1, pieces[0].shape[-1])

    gathered = lax.all_gather(inputs, "tensor", axis=0, tiled=True)
    wide_input = gathered.astype(jnp.float32)
    wide_unit = wide_input * lax.rsqrt(
        jnp.mean(wide_input * wide_input, axis=-1, keepdims=True) + epsilon
    )
    wide_normed = (wide_unit * first_gain).astype(jnp.bfloat16)
    projected = jnp.einsum(
        "td,cdf->ctf", wide_normed, projection, preferred_element_type=jnp.float32
    ).astype(jnp.bfloat16)
    queries = heads_first(projected[0])
    key_rows = heads_first(projected[1])
    value_rows = heads_first(projected[2])
    bucket_hot = (
        bucket_map[None, :] == jnp.arange(bias_table.shape[1], dtype=jnp.int32)[:, None]
    ).astype(jnp.float32)
    offset = 0
    scores = block_scores(queries, key_rows, bias_table, bucket_hot, offset, length, scaling)
    row_peak = jnp.max(scores, axis=-1, keepdims=True)
    shifted = jnp.exp(scores - row_peak)
    row_total = jnp.sum(shifted, axis=-1, keepdims=True)
    weights = (shifted / row_total).astype(jnp.bfloat16)
    log_totals = [row_peak + jnp.log(row_total)]
    context_blocks = jnp.einsum(
        "hqk,hkd->hqd", weights, value_rows, preferred_element_type=jnp.float32
    ).astype(jnp.bfloat16)
    context_flat = heads_last(context_blocks)
    attended = lax.psum_scatter(
        jnp.dot(context_flat, output_weight, preferred_element_type=jnp.float32),
        "tensor",
        scatter_dimension=0,
        tiled=True,
    )
    middle = inputs.astype(jnp.float32) + attended
    second_normed = normalize(middle, second_gain).astype(jnp.bfloat16)
    logits = jnp.dot(second_normed, router_weight, preferred_element_type=jnp.float32)
    expert_ids = jnp.arange(experts, dtype=jnp.int32)
    route_hot = routing[:, :, None] == expert_ids[None, None, :]
    chosen = jnp.sum(jnp.where(route_hot, logits[:, None, :], 0.0), axis=2)
    gate_values = jax.nn.softmax(chosen, axis=-1)
    flat_route = routing.reshape(-1)
    flat_hot = (flat_route[:, None] == expert_ids[None, :]).astype(jnp.int32)
    ranked = jnp.sum(flat_hot * (jnp.cumsum(flat_hot, axis=0, dtype=jnp.int32) - 1), axis=1)
    owner_index = flat_route // local_experts
    within = flat_route % local_experts
    slot_index = (owner_index * capacity + ranked) * local_experts + within
    assign_of = (
        jnp.zeros((slot_count,), jnp.int32)
        .at[slot_index]
        .set(jnp.arange(assignments, dtype=jnp.int32) + 1)
    )
    filled = assign_of > 0
    source_assign = jnp.maximum(assign_of - 1, 0)
    source_token = source_assign // route_count
    send_rows = jnp.where(filled[:, None], second_normed[source_token], jnp.zeros((), jnp.bfloat16))
    upstream = cotangent.astype(jnp.float32)
    gate_flat = gate_values.reshape(-1)
    slot_grad = (jnp.repeat(upstream, route_count, axis=0) * gate_flat[:, None]).astype(
        jnp.bfloat16
    )
    grad_send = jnp.where(filled[:, None], slot_grad[source_assign], jnp.zeros((), jnp.bfloat16))
    arrived = lax.all_to_all(send_rows, "expert", split_axis=0, concat_axis=0, tiled=True)
    expert_rows = lax.all_gather(arrived, "tensor", axis=0, tiled=True)
    row_parts = split_experts(expert_rows)
    pre_parts = [jnp.dot(row_parts[0], expert_up[0], preferred_element_type=jnp.float32)]
    act_parts = [jax.nn.gelu(pre_part).astype(jnp.bfloat16) for pre_part in pre_parts]
    partial_out = join_experts(
        [jnp.dot(act_parts[0], expert_down[0], preferred_element_type=jnp.float32)]
    )
    summed_whole = lax.psum(partial_out.astype(jnp.bfloat16), "tensor").astype(jnp.float32)
    summed = lax.dynamic_slice_in_dim(summed_whole, tensor_index * slot_count, slot_count, 0)
    pre_parts, act_parts, summed = (pre_parts, act_parts, summed.astype(jnp.bfloat16))
    back_rows = lax.all_to_all(summed, "expert", split_axis=0, concat_axis=0, tiled=True)
    grad_arrived = lax.all_to_all(grad_send, "expert", split_axis=0, concat_axis=0, tiled=True)
    grad_gathered = lax.all_gather(grad_arrived, "tensor", axis=0, tiled=True)
    row_parts = split_experts(expert_rows)
    grad_parts = split_experts(grad_gathered)
    number = 0
    down_list = [
        jnp.einsum(
            "rf,rd->fd", act_parts[number], grad_parts[number], preferred_element_type=jnp.float32
        )
    ]
    act_grad = jnp.einsum(
        "rd,fd->rf", grad_parts[number], expert_down[number], preferred_element_type=jnp.float32
    )
    _, gelu_pull = jax.vjp(jax.nn.gelu, pre_parts[number])
    pre_grad = gelu_pull(act_grad)[0].astype(jnp.bfloat16)
    pre_grads = [pre_grad]
    up_list = [
        jnp.einsum("rd,rf->df", row_parts[number], pre_grad, preferred_element_type=jnp.float32)
    ]
    pieces = []
    number = 0
    grad_part = pre_grads[number]
    pieces.append(
        jnp.einsum("rf,df->rd", grad_part, expert_up[number], preferred_element_type=jnp.float32)
    )
    returned_grad = lax.psum_scatter(
        join_experts(pieces).astype(jnp.bfloat16), "tensor", scatter_dimension=0, tiled=True
    ).astype(jnp.float32)
    grad_down, grad_up, returned_grad = (
        jnp.stack(down_list, axis=0),
        jnp.stack(up_list, axis=0),
        returned_grad.astype(jnp.bfloat16),
    )
    coming_back = lax.all_to_all(returned_grad, "expert", split_axis=0, concat_axis=0, tiled=True)
    picked_all = back_rows[slot_index].astype(jnp.float32)
    mixture = gate_values[:, 0:1] * picked_all[0::route_count]
    number = 1
    mixture = mixture + gate_values[:, number : number + 1] * picked_all[number::route_count]
    result = (middle + mixture).astype(jnp.bfloat16)
    gate_grad = jnp.stack(
        [
            jnp.sum(upstream * picked_all[number::route_count], axis=1)
            for number in range(route_count)
        ],
        axis=1,
    )
    coming_all = coming_back[slot_index].astype(jnp.float32)
    normed_grad = coming_all[0::route_count]
    number = 1
    normed_grad = normed_grad + coming_all[number::route_count]
    chosen_grad = gate_values * (
        gate_grad - jnp.sum(gate_values * gate_grad, axis=1, keepdims=True)
    )
    logit_grad = jnp.sum(jnp.where(route_hot, chosen_grad[:, :, None], 0.0), axis=1)
    router_float = router_weight.astype(jnp.float32)
    normed_grad = normed_grad + jnp.dot(logit_grad, router_float.T, precision=highest)
    router_part = jnp.dot(second_normed.astype(jnp.float32).T, logit_grad, precision=highest)
    _, norm_pull = jax.vjp(normalize, middle, second_gain)
    middle_back, second_part = norm_pull(normed_grad)
    middle_grad = upstream + middle_back
    rows_grad = lax.all_gather(middle_grad.astype(jnp.bfloat16), "tensor", axis=0, tiled=True)
    grad_output = jnp.einsum(
        "tw,td->wd", context_flat, rows_grad, preferred_element_type=jnp.float32
    )
    context_grad = jnp.einsum(
        "td,wd->tw", rows_grad, output_weight, preferred_element_type=jnp.float32
    ).astype(jnp.bfloat16)
    context_grad = heads_first(context_grad)
    table_grad = jnp.zeros(bias_table.shape, jnp.float32)
    key_grad = jnp.zeros((heads_here, length, head_size), jnp.float32)
    value_grad = jnp.zeros((heads_here, length, head_size), jnp.float32)
    query_blocks = []
    for number, offset in enumerate(range(0, length, height)):
        scores = block_scores(queries, key_rows, bias_table, bucket_hot, offset, length, scaling)
        weights_full = jnp.exp(scores - log_totals[number])
        prob_grad = jnp.einsum(
            "hqd,hkd->hqk", context_grad, value_rows, preferred_element_type=jnp.float32
        )
        row_dot = jnp.sum(weights_full * prob_grad, axis=-1, keepdims=True)
        score_grad = (weights_full * (prob_grad - row_dot)).astype(jnp.bfloat16)
        value_grad = jnp.einsum(
            "hqk,hqd->hkd",
            weights_full.astype(jnp.bfloat16),
            context_grad,
            preferred_element_type=jnp.float32,
        )
        query_blocks.append(
            scaling
            * jnp.einsum("hqk,hkd->hqd", score_grad, key_rows, preferred_element_type=jnp.float32)
        )
        key_grad = scaling * jnp.einsum(
            "hqk,hqd->hkd", score_grad, queries, preferred_element_type=jnp.float32
        )
        bias_of = partial(
            block_bias, bucket_hot=bucket_hot, offset=offset, height=height, length=length
        )
        _, bias_pull = jax.vjp(bias_of, bias_table)
        table_grad = bias_pull(score_grad.astype(jnp.float32))[0]
    query_grad = query_blocks[0]
    projected_grad = jnp.stack(
        [heads_last(query_grad), heads_last(key_grad), heads_last(value_grad)], axis=0
    ).astype(jnp.bfloat16)
    grad_projection = jnp.einsum(
        "td,ctf->cdf", wide_normed, projected_grad, preferred_element_type=jnp.float32
    )
    wide_grad = jnp.einsum(
        "ctf,cdf->td", projected_grad, projection, preferred_element_type=jnp.float32
    )
    first_part = jnp.sum(wide_grad * wide_unit, axis=0)
    own_grad, first_sum, second_sum, router_sum = (
        lax.psum_scatter(
            wide_grad.astype(jnp.bfloat16), "tensor", scatter_dimension=0, tiled=True
        ).astype(jnp.float32),
        lax.psum_scatter(
            repeated(first_part, tensor_count).astype(jnp.bfloat16),
            "tensor",
            scatter_dimension=0,
            tiled=True,
        ).astype(jnp.float32),
        lax.psum_scatter(
            repeated(second_part, tensor_count).astype(jnp.bfloat16),
            "tensor",
            scatter_dimension=0,
            tiled=True,
        ).astype(jnp.float32),
        lax.psum_scatter(
            repeated(router_part, tensor_count).astype(jnp.bfloat16),
            "tensor",
            scatter_dimension=0,
            tiled=True,
        ).astype(jnp.float32),
    )
    own_input = inputs.astype(jnp.float32)
    _, first_pull = jax.vjp(normalize, own_input, first_gain)
    input_back = first_pull(own_grad)[0]
    grad_inputs = middle_grad + input_back
    dense_totals = lax.psum(
        (grad_projection, grad_output, table_grad, first_sum[0], second_sum[0], router_sum[0]),
        "expert",
    )
    return (
        result,
        grad_inputs,
        dense_totals[0],
        dense_totals[1],
        dense_totals[3],
        dense_totals[4],
        dense_totals[2],
        dense_totals[5],
        grad_up,
        grad_down,
    )


def solution(mesh):
    return jax.shard_map(
        per_device,
        mesh=mesh,
        in_specs=(
            P(("expert", "tensor"), None),
            P(None, None, "tensor"),
            P("tensor", None),
            P(),
            P(),
            P("tensor", None),
            P(),
            P(),
            P(("expert", "tensor"), None),
            P("expert", None, "tensor"),
            P("expert", "tensor", None),
            P(("expert", "tensor"), None),
        ),
        out_specs=(
            P(("expert", "tensor"), None),
            P(("expert", "tensor"), None),
            P(None, None, "tensor"),
            P("tensor", None),
            P(),
            P(),
            P("tensor", None),
            P(),
            P("expert", None, "tensor"),
            P("expert", "tensor", None),
        ),
        check_vma=False,
    )
```

profile of v0, /device:TPU:0, one launch (start us, length us, event | category | flops | bytes accessed | tf_op | source)
XLA Modules:
  0.0 543.4 jit_solution(3805021284912375868)
XLA Ops:
  8.6 10.2 %all_gather.12 = bf16[512,768]{1,0:T(8,128)(2,1)S(1)} all-gather(bf16[128,768]{1,0:T(8,128)(2,1)} %param.12), channel_id=1, replica_groups=mesh['expert'=8,'tensor'=4] {'tensor'}, dimensions={0}, use_global_device_ids=true | all-gather | bytes 983040 | tf_op jit(solution)/shard_map/all_gather | solution.py:86
  19.1 1.9 fusion.39
  21.2 3.5 broadcast_bitcast_fusion
  24.8 10.4 %copy.71 = f32[1,3,513,1024]{3,1,2,0:T(4,128)} copy(f32[1,3,513,1024]{3,2,1,0:T(8,128)} %broadcast_bitcast_fusion) | data formatting | bytes 12607488
  35.1 9.4 %slice.67 = f32[3,523776]{1,0:T(4,128)} slice(f32[3,525312]{1,0:T(4,128)} %bitcast.118), slice={[0:3], [511:524287]} | slice | bytes 12570624 | tf_op jit(solution)/shard_map/slice | solution.py:24
  44.6 13.2 %reshape.280 = f32[3,512,1023]{2,1,0:T(8,128)} reshape(f32[3,523776]{1,0:T(4,128)} %slice.67) | data formatting | bytes 12570624 | tf_op jit(solution)/shard_map/reshape | solution.py:25
  57.8 3.9 slice.68
  61.6 3.5 copy.69
  65.1 2.8 fusion.60
  74.8 25.6 %reduce-scatter.5.cloned.1.call-done = f32[128,768]{1,0:T(8,128)} async-done(((f32[512,768]{1,0:T(8,128)}), f32[128,768]{1,0:T(8,128)}) %reduce-scatter.5.cloned.1.call-update) | async-done | bytes 393232 | tf_op jit(solution)/shard_map/reduce_scatter | solution.py:112
  101.7 2.2 gather_fusion
  104.0 22.0 %all_to_all.42 = bf16[8,48,768]{2,1,0:T(8,128)(2,1)} all-to-all(bf16[8,48,768]{2,1,0:T(8,128)(2,1)S(1)} %broadcast_select_fusion.1), channel_id=1, replica_groups=mesh['expert'=8,'tensor'=4] {'expert'}, dimensions={0} | all-to-all | bytes 1179648 | tf_op jit(solution)/shard_map/all_to_all | solution.py:146
  126.0 21.6 %all-gather.3.cloned.1.call-done = bf16[1536,768]{1,0:T(8,128)(2,1)} async-done(((bf16[384,768]{1,0:T(8,128)(2,1)}), bf16[1536,768]{1,0:T(8,128)(2,1)}) %all-gather.3.cloned.1.call-update) | async-done | bytes 2359312 | tf_op jit(solution)/shard_map/all_gather | solution.py:147
  147.7 4.0 fusion.24
  151.7 2.1 copy-done.56
  153.8 4.4 convolution_convert_fusion.1
  158.2 55.8 %all-reduce.11.cloned.1.call-done = bf16[1536,768]{1,0:T(8,128)(2,1)} async-done(((bf16[1536,768]{1,0:T(8,128)(2,1)}), bf16[1536,768]{1,0:T(8,128)(2,1)}) %all-reduce.11.cloned.1.call-update) | async-done | bytes 2359312 | tf_op jit(solution)/shard_map/psum | solution.py:154
  214.0 1.9 convert_convert_fusion
  215.9 5.5 %all-to-all-start.1 = ((bf16[8,48,768]{2,1,0:T(8,128)(2,1)}), bf16[8,48,768]{2,1,0:T(8,128)(2,1)S(1)}, u32[]{:S(2)}, u32[]{:S(2)}) async-start(bf16[8,48,768]{2,1,0:T(8,128)(2,1)} %bitcast.22), calls=%async_computation.2 | async-start | bytes 1179648 | tf_op jit(solution)/shard_map/all_to_all | solution.py:157
  223.4 13.9 %all-to-all-done.1 = bf16[8,48,768]{2,1,0:T(8,128)(2,1)S(1)} async-done(((bf16[8,48,768]{2,1,0:T(8,128)(2,1)}), bf16[8,48,768]{2,1,0:T(8,128)(2,1)S(1)}, u32[]{:S(2)}, u32[]{:S(2)}) %all-to-all-start.1) | async-done | bytes 589856 | tf_op jit(solution)/shard_map/all_to_all | solution.py:157
  241.0 2.2 gather_fusion.2
  243.4 20.2 %all_to_all.43 = bf16[8,48,768]{2,1,0:T(8,128)(2,1)} all-to-all(bf16[8,48,768]{2,1,0:T(8,128)(2,1)S(1)} %broadcast_select_fusion), channel_id=1, replica_groups=mesh['expert'=8,'tensor'=4] {'expert'}, dimensions={0} | all-to-all | bytes 1179648 | tf_op jit(solution)/shard_map/all_to_all | solution.py:158
  263.9 21.7 %all-gather.5.cloned.1.call-done = bf16[1536,768]{1,0:T(8,128)(2,1)} async-done(((bf16[384,768]{1,0:T(8,128)(2,1)}), bf16[1536,768]{1,0:T(8,128)(2,1)}) %all-gather.5.cloned.1.call-update) | async-done | bytes 2359312 | tf_op jit(solution)/shard_map/all_gather | solution.py:159
  285.6 7.6 %fusion.6 = bf16[1536,768]{1,0:T(8,128)(2,1)S(1)} fusion(f32[1536,768]{1,0:T(8,128)} %copy-done.56, bf16[1536,768]{1,0:T(8,128)(2,1)} %all-gather.5.cloned.1.call-done, bf16[1,768,768]{2,1,0:T(8,128)(2,1)S(1)} %copy-done), kind=kOutput, calls=%fused_computation.13 | convolution fusion | flops 1835532288 | bytes 10616832 | tf_op jit(solution)/shard_map/rd,fd->rf/dot_general | solution.py:168
  294.6 3.4 convolution_convert_fusion
  298.1 33.2 %reduce-scatter.7.cloned.1.call-done = bf16[384,768]{1,0:T(8,128)(2,1)} async-done(((bf16[1536,768]{1,0:T(8,128)(2,1)}), bf16[384,768]{1,0:T(8,128)(2,1)}) %reduce-scatter.7.cloned.1.call-update) | async-done | bytes 589840 | tf_op jit(solution)/shard_map/reduce_scatter | solution.py:183
  331.3 5.5 %all-to-all-start.3 = ((bf16[8,48,768]{2,1,0:T(8,128)(2,1)}), bf16[8,48,768]{2,1,0:T(8,128)(2,1)S(1)}, u32[]{:S(2)}, u32[]{:S(2)}) async-start(bf16[8,48,768]{2,1,0:T(8,128)(2,1)} %bitcast.136), calls=%async_computation.5 | async-start | bytes 1179648 | tf_op jit(solution)/shard_map/all_to_all | solution.py:191
  339.0 21.2 %reduce-scatter.11.cloned.1.call-done = bf16[1,768,8]{1,2,0:T(8,128)(2,1)} async-done(((bf16[4,768,8]{1,2,0:T(8,128)(2,1)}), bf16[1,768,8]{1,2,0:T(8,128)(2,1)}) %reduce-scatter.11.cloned.1.call-update) | async-done | bytes 12304 | tf_op jit(solution)/shard_map/reduce_scatter | solution.py:283
  361.5 1.9 gather_fusion.3
  363.5 3.1 slice.54
  366.6 3.0 slice.55
  369.6 2.3 multiply_reduce_fusion.1
  374.2 7.9 %all_gather.15 = bf16[512,768]{1,0:T(8,128)(2,1)S(1)} all-gather(bf16[128,768]{1,0:T(8,128)(2,1)S(1)} %fusion.57), channel_id=1, replica_groups=mesh['expert'=8,'tensor'=4] {'tensor'}, dimensions={0}, use_global_device_ids=true | all-gather | bytes 983040 | tf_op jit(solution)/shard_map/all_gather | solution.py:218
  387.5 2.2 bitcast_convert_fusion
  390.1 5.3 convolution_bitcast_fusion.1
  395.3 6.5 %convolution_bitcast_fusion = f32[1,768,768]{2,1,0:T(8,128)} fusion(bf16[1536,768]{1,0:T(8,128)(2,1)S(1)} %copy-done.51, f32[1536,768]{1,0:T(8,128)} %copy-done.56), kind=kOutput, calls=%fused_computation.31 | convolution fusion | flops 1822556160 | bytes 9437184 | tf_op jit(solution)/shard_map/rf,rd->fd/dot_general | solution.py:164
  403.4 1.8 pad.9.clone
  405.2 7.4 %reshape.347 = bf16[1571328]{0:T(1024)(128)(2,1)} reshape(bf16[3,512,1023]{2,1,0:T(8,128)(2,1)S(1)} %pad.9.clone) | data formatting | bytes 6285312
  412.7 5.7 %reshape.285 = bf16[3,523776]{1,0:T(4,128)(2,1)} reshape(bf16[1571328]{0:T(1024)(128)(2,1)} %reshape.347) | data formatting | bytes 6285312 | tf_op jit(solution)/shard_map/transpose(jvp())/reshape | solution.py:25
  419.6 2.0 convolution_bitcast_fusion.2
  421.6 7.8 %pad_convert_fusion = f32[3,525312]{1,0:T(4,128)} fusion(bf16[3,523776]{1,0:T(4,128)(2,1)} %reshape.285), kind=kLoop, calls=%fused_computation.15 | loop fusion | flops 1575936 | bytes 9446400 | tf_op jit(solution)/shard_map/transpose(jvp())/reshape | solution.py:22
  429.5 10.8 %reshape.291 = f32[3,513,1024]{2,1,0:T(8,128)} reshape(f32[3,525312]{1,0:T(4,128)} %pad_convert_fusion) | data formatting | bytes 12607488 | tf_op jit(solution)/shard_map/transpose(jvp())/reshape | solution.py:22
  440.3 3.4 reduce_sum.188
  445.8 12.1 %all-reduce.7 = (bf16[4,768]{1,0:T(4,128)(2,1)S(1)}, bf16[4,768]{1,0:T(4,128)(2,1)S(1)}) all-reduce(bf16[4,768]{1,0:T(4,128)(2,1)S(1)} %broadcast_in_dim.134, bf16[4,768]{1,0:T(4,128)(2,1)S(1)} %broadcast_in_dim.135), channel_id=5, replica_groups=mesh['expert'=8,'tensor'=4] {'tensor'}, use_global_device_ids=true, to_apply=%region_26.27.clone | all-reduce | flops 6144 | bytes 24576
  459.4 38.0 %all-reduce.5 = (f32[768]{0:T(1024)}, f32[768]{0:T(1024)}, f32[3,32]{1,0:T(4,128)}, f32[768,8]{0,1:T(8,128)}) all-reduce(f32[768]{0:T(1024)S(1)} %fusion.47, f32[768]{0:T(1024)S(1)} %fusion.46, f32[3,32]{1,0:T(4,128)S(1)} %fusion.41, f32[768,8]{0,1:T(8,128)S(1)} %copy-done.39), channel_id=1, replica_groups=mesh['expert'=8,'tensor'=4] {'expert'}, use_global_device_ids=true, to_apply=%region_27.28 | all-reduce | flops 7776 | bytes 62208 | tf_op jit(solution)/shard_map/psum | solution.py:294
  498.6 2.1 fusion.34
  500.7 31.7 %all-reduce.13.cloned.1.call-done = (f32[3,768,192]{1,2,0:T(8,128)}, f32[192,768]{1,0:T(8,128)}) async-done(((f32[3,768,192]{1,2,0:T(8,128)}, f32[192,768]{1,0:T(8,128)}), (f32[3,768,192]{1,2,0:T(8,128)}, f32[192,768]{1,0:T(8,128)})) %all-reduce.13.cloned.1.call-update) | async-done | bytes 2359312 | tf_op jit(solution)/shard_map/psum | solution.py:294
  532.4 2.9 copy.75
  (210 shorter events, 37.1 us)
Async XLA Ops:
  7.2 146.6 %copy-start = (bf16[1,768,768]{2,1,0:T(8,128)(2,1)S(1)}, bf16[1,768,768]{2,1,0:T(8,128)(2,1)}, u32[]{:S(2)}) copy-start(bf16[1,768,768]{2,1,0:T(8,128)(2,1)} %param.22) | copy-start | bytes 3538948
  7.2 93.2 %reduce-scatter.5.cloned.1.call-start = ((), (), s32[]{:S(2)}) async-start(), calls=%async_computation.8 | async-start | bytes 1966080 | tf_op jit(solution)/shard_map/reduce_scatter | solution.py:112
  21.2 43.9 %copy-start.22 = (bf16[1,512,192]{1,2,0:T(8,128)(2,1)}, bf16[1,512,192]{1,2,0:T(8,128)(2,1)S(1)}, u32[]{:S(2)}) copy-start(bf16[1,512,192]{1,2,0:T(8,128)(2,1)S(1)} %get-tuple-element.28) | copy-start | bytes 589828
  21.2 43.9 %copy-start.24 = (bf16[1,512,192]{1,2,0:T(8,128)(2,1)}, bf16[1,512,192]{1,2,0:T(8,128)(2,1)S(1)}, u32[]{:S(2)}) copy-start(bf16[1,512,192]{1,2,0:T(8,128)(2,1)S(1)} %get-tuple-element.30) | copy-start | bytes 589828
  21.2 47.1 %copy-start.28 = (bf16[1,512,192]{1,2,0:T(8,128)(2,1)}, bf16[1,512,192]{1,2,0:T(8,128)(2,1)S(1)}, u32[]{:S(2)}) copy-start(bf16[1,512,192]{1,2,0:T(8,128)(2,1)S(1)} %get-tuple-element.29) | copy-start | bytes 589828
  69.6 32.1 %copy-start.30 = (bf16[3,512,64]{1,2,0:T(8,128)(2,1)}, bf16[3,512,64]{1,2,0:T(8,128)(2,1)S(1)}, u32[]{:S(2)}) copy-start(bf16[3,512,64]{1,2,0:T(8,128)(2,1)S(1)} %fusion.28) | copy-start | bytes 589828
  69.6 30.8 %copy-start.16 = (bf16[128,768]{1,0:T(8,128)(2,1)S(1)}, bf16[128,768]{1,0:T(8,128)(2,1)}, u32[]{:S(2)}) copy-start(bf16[128,768]{1,0:T(8,128)(2,1)} %param.12) | copy-start | bytes 589828
  69.6 32.0 %copy-start.40 = (f32[768]{0:T(1024)S(1)}, f32[768]{0:T(1024)}, u32[]{:S(2)}) copy-start(f32[768]{0:T(1024)} %param.16) | copy-start | bytes 9220
  71.2 76.5 %all-gather.3.cloned.1.call-start = ((), (), s32[]{:S(2)}) async-start(), calls=%async_computation.9 | async-start | bytes 2949120 | tf_op jit(solution)/shard_map/all_gather | solution.py:147
  126.0 88.0 %all-reduce.11.cloned.1.call-start = ((), (), s32[]{:S(2)}) async-start(), calls=%async_computation.10 | async-start | bytes 4718592 | tf_op jit(solution)/shard_map/psum | solution.py:154
  158.2 63.3 %copy-start.18 = (bf16[128,768]{1,0:T(8,128)(2,1)S(1)}, bf16[128,768]{1,0:T(8,128)(2,1)}, u32[]{:S(2)}) copy-start(bf16[128,768]{1,0:T(8,128)(2,1)} %param.23) | copy-start | bytes 589828
  158.2 65.0 %copy-start.41 = (bf16[768,8]{0,1:T(8,128)(2,1)S(1)}, bf16[768,8]{0,1:T(8,128)(2,1)}, u32[]{:S(2)}) copy-start(bf16[768,8]{0,1:T(8,128)(2,1)} %param.19) | copy-start | bytes 36868
  215.9 21.3 %all-to-all-start.1 = ((bf16[8,48,768]{2,1,0:T(8,128)(2,1)}), bf16[8,48,768]{2,1,0:T(8,128)(2,1)S(1)}, u32[]{:S(2)}, u32[]{:S(2)}) async-start(bf16[8,48,768]{2,1,0:T(8,128)(2,1)} %bitcast.22), calls=%async_computation.2 | async-start | bytes 1179648 | tf_op jit(solution)/shard_map/all_to_all | solution.py:157
  221.5 64.1 %all-gather.5.cloned.1.call-start = ((), (), s32[]{:S(2)}) async-start(), calls=%async_computation.11 | async-start | bytes 2949120 | tf_op jit(solution)/shard_map/all_gather | solution.py:159
  239.3 3.9 copy-start.12
  263.6 31.0 %copy-start.52 = (bf16[1,768,768]{2,1,0:T(8,128)(2,1)S(1)}, bf16[1,768,768]{2,1,0:T(8,128)(2,1)}, u32[]{:S(2)}) copy-start(bf16[1,768,768]{2,1,0:T(8,128)(2,1)} %param.21) | copy-start | bytes 3538948
  263.6 67.6 %reduce-scatter.7.cloned.1.call-start = ((), (), s32[]{:S(2)}) async-start(), calls=%async_computation.12 | async-start | bytes 2949120 | tf_op jit(solution)/shard_map/reduce_scatter | solution.py:183
  298.0 38.8 %copy-start.55 = (u32[32]{0:T(128)S(1)}, u32[32]{0:T(128)}, u32[]{:S(2)}) copy-start(u32[32]{0:T(128)} %constant.115) | copy-start | bytes 388
  331.3 30.3 %all-to-all-start.3 = ((bf16[8,48,768]{2,1,0:T(8,128)(2,1)}), bf16[8,48,768]{2,1,0:T(8,128)(2,1)S(1)}, u32[]{:S(2)}, u32[]{:S(2)}) async-start(bf16[8,48,768]{2,1,0:T(8,128)(2,1)} %bitcast.136), calls=%async_computation.5 | async-start | bytes 1179648 | tf_op jit(solution)/shard_map/all_to_all | solution.py:191
  336.8 23.4 %reduce-scatter.11.cloned.1.call-start = ((), (), s32[]{:S(2)}) async-start(), calls=%async_computation.14 | async-start | bytes 61440 | tf_op jit(solution)/shard_map/reduce_scatter | solution.py:283
  338.4 159.0 %reduce-scatter.9.cloned.1.call-start = ((), (), s32[]{:S(2)}) async-start(), calls=%async_computation.13 | async-start | bytes 983040 | tf_op jit(solution)/shard_map/reduce_scatter | solution.py:268
  363.5 19.9 %copy-start.3 = (f32[3,512,512]{1,2,0:T(8,128)S(1)}, f32[3,512,512]{1,2,0:T(8,128)}, u32[]{:S(2)}) copy-start(f32[3,512,512]{1,2,0:T(8,128)} %copy-done.2) | copy-start | bytes 9437188
  369.6 13.4 %copy-start.27 = (bf16[192,768]{1,0:T(8,128)(2,1)S(1)}, bf16[192,768]{1,0:T(8,128)(2,1)}, u32[]{:S(2)}) copy-start(bf16[192,768]{1,0:T(8,128)(2,1)} %param.14) | copy-start | bytes 884740
  374.2 9.8 %copy-start.29 = (bf16[1,512,192]{1,2,0:T(8,128)(2,1)S(1)}, bf16[1,512,192]{1,2,0:T(8,128)(2,1)}, u32[]{:S(2)}) copy-start(bf16[1,512,192]{1,2,0:T(8,128)(2,1)} %copy-done.28) | copy-start | bytes 589828
  385.7 4.1 copy-start.4
  386.3 3.5 copy-start.35
  386.3 3.7 copy-start.20
  389.8 142.7 %all-reduce.13.cloned.1.call-start = ((), (), s32[]{:S(2)}) async-start(), calls=%async_computation.15 | async-start | bytes 4718592 | tf_op jit(solution)/shard_map/psum | solution.py:294
  390.1 5.3 copy-start.51
  395.3 6.5 %copy-start.5 = (bf16[3,512,512]{1,2,0:T(8,128)(2,1)S(1)}, bf16[3,512,512]{1,2,0:T(8,128)(2,1)}, u32[]{:S(2)}) copy-start(bf16[3,512,512]{1,2,0:T(8,128)(2,1)} %copy-done.4) | copy-start | bytes 4718596
  412.6 5.8 %copy-start.7 = (bf16[512,768]{1,0:T(8,128)(2,1)S(1)}, bf16[512,768]{1,0:T(8,128)(2,1)}, u32[]{:S(2)}) copy-start(bf16[512,768]{1,0:T(8,128)(2,1)} %copy-done.6) | copy-start | bytes 2359300
  412.6 5.8 %copy-start.31 = (bf16[3,512,64]{1,2,0:T(8,128)(2,1)S(1)}, bf16[3,512,64]{1,2,0:T(8,128)(2,1)}, u32[]{:S(2)}) copy-start(bf16[3,512,64]{1,2,0:T(8,128)(2,1)} %copy-done.30) | copy-start | bytes 589828
  412.6 6.9 %copy-start.9 = (bf16[512,768]{1,0:T(8,128)(2,1)S(1)}, bf16[512,768]{1,0:T(8,128)(2,1)}, u32[]{:S(2)}) copy-start(bf16[512,768]{1,0:T(8,128)(2,1)} %copy-done.8) | copy-start | bytes 2359300
  412.6 6.9 %copy-start.34 = (bf16[3,512,64]{1,2,0:T(8,128)(2,1)S(1)}, bf16[3,512,64]{1,2,0:T(8,128)(2,1)}, u32[]{:S(2)}) copy-start(bf16[3,512,64]{1,2,0:T(8,128)(2,1)} %copy-done.33) | copy-start | bytes 589828
  412.6 6.9 %copy-start.36 = (bf16[3,512,64]{1,2,0:T(8,128)(2,1)S(1)}, bf16[3,512,64]{1,2,0:T(8,128)(2,1)}, u32[]{:S(2)}) copy-start(bf16[3,512,64]{1,2,0:T(8,128)(2,1)} %copy-done.35) | copy-start | bytes 589828
  412.7 6.9 %copy-start.38 = (bf16[3,512,64]{1,2,0:T(8,128)(2,1)S(1)}, bf16[3,512,64]{1,2,0:T(8,128)(2,1)}, u32[]{:S(2)}) copy-start(bf16[3,512,64]{1,2,0:T(8,128)(2,1)} %copy-done.37) | copy-start | bytes 589828
  412.7 6.9 %copy-start.42 = (f32[768]{0:T(1024)S(1)}, f32[768]{0:T(1024)}, u32[]{:S(2)}) copy-start(f32[768]{0:T(1024)} %param.15) | copy-start | bytes 9220
  412.7 6.9 %copy-start.45 = (f32[512]{0:T(512)S(1)}, f32[512]{0:T(512)}, u32[]{:S(2)}) copy-start(f32[512]{0:T(512)} %copy-done.44) | copy-start | bytes 6148
  440.2 3.8 copy-start.46
  440.2 5.5 %copy-start.47 = (bf16[768]{0:T(1024)(128)(2,1)S(1)}, bf16[768]{0:T(1024)(128)(2,1)}, u32[]{:S(2)}) copy-start(bf16[768]{0:T(1024)(128)(2,1)} %get-tuple-element.10) | copy-start | bytes 4612
  440.2 19.0 %copy-start.54 = (s32[512]{0:T(512)S(1)}, s32[512]{0:T(512)}, u32[]{:S(2)}) copy-start(s32[512]{0:T(512)} %param.18) | copy-start | bytes 6148
  440.2 19.2 %copy-start.39 = (f32[768,8]{0,1:T(8,128)S(1)}, f32[768,8]{0,1:T(8,128)}, u32[]{:S(2)}) copy-start(f32[768,8]{0,1:T(8,128)} %bitcast_convert_fusion.1) | copy-start | bytes 73732
  440.2 57.2 %copy-start.17 = (bf16[128,768]{1,0:T(8,128)(2,1)S(1)}, bf16[128,768]{1,0:T(8,128)(2,1)}, u32[]{:S(2)}) copy-start(bf16[128,768]{1,0:T(8,128)(2,1)} %param.12) | copy-start | bytes 589828
  440.3 58.3 %copy-start.11 = (f32[128,768]{1,0:T(8,128)S(1)}, f32[128,768]{1,0:T(8,128)}, u32[]{:S(2)}) copy-start(f32[128,768]{1,0:T(8,128)} %copy-done.10) | copy-start | bytes 1179652
  440.3 58.3 %copy-start.13 = (f32[128,768]{1,0:T(8,128)S(1)}, f32[128,768]{1,0:T(8,128)}, u32[]{:S(2)}) copy-start(f32[128,768]{1,0:T(8,128)} %copy-done.12) | copy-start | bytes 1179652
  440.3 58.3 %copy-start.15 = (f32[128,768]{1,0:T(8,128)S(1)}, f32[128,768]{1,0:T(8,128)}, u32[]{:S(2)}) copy-start(f32[128,768]{1,0:T(8,128)} %copy-done.14) | copy-start | bytes 1179652
  440.3 58.3 %copy-start.19 = (bf16[128,768]{1,0:T(8,128)(2,1)S(1)}, bf16[128,768]{1,0:T(8,128)(2,1)}, u32[]{:S(2)}) copy-start(bf16[128,768]{1,0:T(8,128)(2,1)} %param.23) | copy-start | bytes 589828
  498.5 37.6 %copy-start.1 = (bf16[1,768,768]{2,1,0:T(8,128)(2,1)S(1)}, bf16[1,768,768]{2,1,0:T(8,128)(2,1)}, u32[]{:S(2)}) copy-start(bf16[1,768,768]{2,1,0:T(8,128)(2,1)} %param.22) | copy-start | bytes 3538948
  (19 other events, 33.1 us)
Sparse Core Ops, SparseCore 0:
  71.3 29.0 reduce-scatter.4
  126.1 21.5 all-gather.2
  158.3 55.6 all-reduce.10
  263.8 21.7 all-gather.4
  298.2 33.0 reduce-scatter.6
  340.3 19.8 reduce-scatter.10
  389.9 24.1 reduce-scatter.8
  421.7 110.6 all-reduce.12
where the time goes:
time: 550 us; the launch traced here: 543 us
  waiting for transfers between devices  225 us (41%)
  blocking collectives  110 us (20%)
  local copies, waits for them, and re-layouts  103 us (19%)
  matrix products  49.8 us (9%)
  other arithmetic  27.9 us (5%)
  between operations  15.4 us (3%)
  starting transfers between devices  11.7 us (2%)
    psum x1, waiting for transfers between devices, per_device(): lax.psum(partial_out.astype(jnp.bfloat16), 'tensor').astype(jnp.float32)  55.8 us
    psum x1, blocking collectives, per_device(): lax.psum((grad_projection, grad_output, table_grad, first_sum[0], second_...  38 us
    unnamed x123, local copies, waits for them, and re-layouts  37.4 us
    reduce_scatter x1, waiting for transfers between devices, per_device(): lax.psum_scatter(join_experts(pieces).astype(jnp.bfloat16), 'tensor', sca...  33.2 us
    psum x1, waiting for transfers between devices, per_device(): lax.psum((grad_projection, grad_output, table_grad, first_sum[0], second_...  31.7 us
    reduce_scatter x1, waiting for transfers between devices, per_device(): lax.psum_scatter(jnp.dot(context_flat, output_weight, preferred_element_t...  25.6 us
    all_to_all x1, blocking collectives, per_device(): lax.all_to_all(send_rows, 'expert', split_axis=0, concat_axis=0, tiled=True)  22 us
    all_gather x1, waiting for transfers between devices, per_device(): grad_gathered = lax.all_gather(grad_arrived, 'tensor', axis=0, tiled=True)  21.7 us
  transfers between devices with their start and end apart: 10, of which 8 were waited for; matrix products, arithmetic and copies ran while one was open for 13% of the time, Pallas kernels for 0%

commit v1 on v0

v1 whole, which is shorter than its diff:
```python
from functools import partial

import jax
import jax.numpy as jnp
from jax import lax
from jax.experimental import pallas as pl
from jax.experimental.pallas import tpu as pltpu
from jax.sharding import PartitionSpec as P

epsilon = 1e-06
negative = -1e30
highest = lax.Precision.HIGHEST
f32 = jnp.float32
bf16 = jnp.bfloat16
MESH = pl.DeviceIdType.MESH
limit = 50 * 1024 * 1024


def dot(left, right):
    return jnp.dot(left, right, preferred_element_type=f32)


def dot_nt(left, right):
    return lax.dot_general(left, right, (((1,), (1,)), ((), ())), preferred_element_type=f32)


def dot_tn(left, right):
    return lax.dot_general(left, right, (((0,), (0,)), ((), ())), preferred_element_type=f32)


def vmem(count):
    return [pl.BlockSpec(memory_space=pltpu.VMEM)] * count


def dma(*shape):
    return pltpu.SemaphoreType.DMA(shape)


def params(number):
    return pltpu.CompilerParams(
        collective_id=number, has_side_effects=True, vmem_limit_bytes=limit
    )


def remote(source, target, send, recv, where):
    return pltpu.make_async_remote_copy(
        src_ref=source,
        dst_ref=target,
        send_sem=send,
        recv_sem=recv,
        device_id=where,
        device_id_type=MESH,
    )


def greet(places):
    barrier = pltpu.get_barrier_semaphore()
    for where in places:
        pl.semaphore_signal(barrier, inc=1, device_id=where, device_id_type=MESH)
    pl.semaphore_wait(barrier, len(places))


def tensor_partners():
    me = lax.axis_index("tensor")
    core = lax.rem(me, 2)
    return me, core, me + 1 - 2 * core, lax.rem(me + 2, 4)


def gather_kernel(x_ref, o_ref, send, recv, local):
    me, core, near, far = tensor_partners()
    corner = lax.rem(near + 2, 4)
    to_near, to_far = {"tensor": near}, {"tensor": far}
    greet([to_near, to_far])
    copy_far = remote(x_ref, o_ref.at[me], send.at[1], recv.at[1], to_far)
    copy_far.start()
    copy_near = remote(x_ref, o_ref.at[me], send.at[0], recv.at[0], to_near)
    copy_near.start()
    own = pltpu.make_async_copy(x_ref, o_ref.at[me], local)
    own.start()
    remote(x_ref, o_ref.at[far], send.at[1], recv.at[1], to_far).wait_recv()
    relay = remote(o_ref.at[far], o_ref.at[far], send.at[2], recv.at[2], to_near)
    relay.start()
    remote(x_ref, o_ref.at[near], send.at[0], recv.at[0], to_near).wait_recv()
    remote(x_ref, o_ref.at[corner], send.at[2], recv.at[2], to_near).wait_recv()
    own.wait()
    copy_far.wait_send()
    copy_near.wait_send()
    relay.wait_send()


def gather_tensor(rows, number):
    height, width = rows.shape
    return pl.pallas_call(
        gather_kernel,
        out_shape=jax.ShapeDtypeStruct((4, height, width), rows.dtype),
        in_specs=vmem(1),
        out_specs=vmem(1)[0],
        scratch_shapes=[dma(3), dma(3), pltpu.SemaphoreType.DMA],
        compiler_params=params(number),
    )(rows).reshape(4 * height, width)


def scatter_kernel(x_ref, o_ref, got, mid, came, send, recv):
    me, core, near, far = tensor_partners()
    side = me // 2
    to_near, to_far = {"tensor": near}, {"tensor": far}
    greet([to_near, to_far])
    swaps = []
    for part in (0, 1):
        at_x = lax.rem(side + 1 + part, 2)
        swap = remote(
            x_ref.at[at_x, 1 - core], got.at[part], send.at[part], recv.at[part], to_near
        )
        swap.start()
        swaps.append(swap)
    swaps[0].wait_recv()
    mid[...] = (x_ref[1 - side, core].astype(f32) + got[0].astype(f32)).astype(mid.dtype)
    cross = remote(mid, came, send.at[2], recv.at[2], to_far)
    cross.start()
    swaps[1].wait_recv()
    total = x_ref[side, core].astype(f32) + got[1].astype(f32)
    cross.wait_recv()
    o_ref[...] = total + came[...].astype(f32)
    swaps[0].wait_send()
    swaps[1].wait_send()
    cross.wait_send()


def scatter_tensor(rows, number):
    height, width = rows.shape[0] // 4, rows.shape[1]
    return pl.pallas_call(
        scatter_kernel,
        out_shape=jax.ShapeDtypeStruct((height, width), f32),
        in_specs=vmem(1),
        out_specs=vmem(1)[0],
        scratch_shapes=[
            pltpu.VMEM((2, height, width), rows.dtype),
            pltpu.VMEM((height, width), rows.dtype),
            pltpu.VMEM((height, width), rows.dtype),
            dma(3),
            dma(3),
        ],
        compiler_params=params(number),
    )(rows.reshape(2, 2, height, width))


def dispatch_kernel(groups, x_ref, o_ref, es, er, bs, br, ns, nr, cs, cr, local):
    me, core, near, far = tensor_partners()
    corner = lax.rem(near + 2, 4)
    mine = lax.axis_index("expert")
    to_near, to_far = {"tensor": near}, {"tensor": far}
    greet([{"expert": lax.rem(mine + k, groups)} for k in range(1, groups)] + [to_near, to_far])
    own = pltpu.make_async_copy(x_ref.at[:, mine], o_ref.at[:, me, mine], local)
    own.start()
    sends = []
    for k in range(1, groups):
        there = lax.rem(mine + k, groups)
        copy = remote(
            x_ref.at[:, there], o_ref.at[:, me, mine], es.at[k], er.at[k], {"expert": there}
        )
        copy.start()
        sends.append(copy)

    def source(k):
        return lax.rem(mine + groups - k, groups)

    def relay(k):
        place = source(k)
        block = o_ref.at[:, far, place]
        remote(block, block, bs.at[k], br.at[k], to_far).wait_recv()
        copy = remote(block, block, cs.at[k], cr.at[k], to_near)
        copy.start()
        sends.append(copy)

    for k in range(groups):
        place = source(k)
        block = o_ref.at[:, me, place]
        if k == 0:
            own.wait()
        else:
            remote(x_ref.at[:, place], block, es.at[k], er.at[k], {"expert": place}).wait_recv()
        copy = remote(block, block, bs.at[k], br.at[k], to_far)
        copy.start()
        sends.append(copy)
        copy = remote(block, block, ns.at[k], nr.at[k], to_near)
        copy.start()
        sends.append(copy)
        if k > 0:
            relay(k - 1)
    relay(groups - 1)
    for k in range(groups):
        place = source(k)
        block = o_ref.at[:, near, place]
        remote(block, block, ns.at[k], nr.at[k], to_near).wait_recv()
        block = o_ref.at[:, corner, place]
        remote(block, block, cs.at[k], cr.at[k], to_near).wait_recv()
    for copy in sends:
        copy.wait_send()


def dispatch(rows, number):
    kinds, groups, height, width = rows.shape
    return pl.pallas_call(
        partial(dispatch_kernel, groups),
        out_shape=jax.ShapeDtypeStruct((kinds, 4, groups, height, width), rows.dtype),
        in_specs=[pl.BlockSpec(memory_space=pl.ANY)],
        out_specs=pl.BlockSpec(memory_space=pl.ANY),
        scratch_shapes=[dma(groups)] * 8 + [pltpu.SemaphoreType.DMA],
        compiler_params=params(number),
    )(rows)


def collect_kernel(groups, p_ref, g_ref, o_ref, got, mid, came, done, ps, pr, xs, xr, es, er):
    me, core, near, far = tensor_partners()
    side = me // 2
    mine = lax.axis_index("expert")
    to_near, to_far = {"tensor": near}, {"tensor": far}
    greet([{"expert": lax.rem(mine + k, groups)} for k in range(1, groups)] + [to_near, to_far])
    order = list(range(1, groups)) + [0]
    refs = (p_ref, g_ref)
    swaps, sends = {}, []
    for k in order:
        there = lax.rem(mine + k, groups)
        for kind in (0, 1):
            copy = remote(
                refs[kind].at[:, 1 - core, there],
                got.at[kind, :, k],
                ps.at[kind, k],
                pr.at[kind, k],
                to_near,
            )
            copy.start()
            swaps[kind, k] = copy
    crosses = {}

    def finish(k):
        there = lax.rem(mine + k, groups)
        crosses[k].wait_recv()
        for kind in (0, 1):
            total = (
                refs[kind][side, core, there].astype(f32)
                + got[kind, side, k].astype(f32)
                + came[k, kind].astype(f32)
            ).astype(bf16)
            if k:
                done[k, kind] = total
            else:
                o_ref[kind, mine] = total
        if k:
            copy = remote(
                done.at[k], o_ref.at[:, mine], es.at[k], er.at[k], {"expert": there}
            )
            copy.start()
            sends.append(copy)

    for at, k in enumerate(order):
        there = lax.rem(mine + k, groups)
        for kind in (0, 1):
            swaps[kind, k].wait_recv()
            mid[k, kind] = (
                refs[kind][1 - side, core, there].astype(f32)
                + got[kind, 1 - side, k].astype(f32)
            ).astype(bf16)
        copy = remote(mid.at[k], came.at[k], xs.at[k], xr.at[k], to_far)
        copy.start()
        crosses[k] = copy
        if at > 1:
            finish(order[at - 2])
    finish(order[-2])
    finish(order[-1])
    for k in range(1, groups):
        place = lax.rem(mine + groups - k, groups)
        remote(done.at[k], o_ref.at[:, place], es.at[k], er.at[k], {"expert": place}).wait_recv()
    for copy in list(swaps.values()) + list(crosses.values()) + sends:
        copy.wait_send()


def collect(first, second, groups, number):
    height, width = first.shape[0] // (4 * groups), first.shape[1]
    view = (2, 2, groups, height, width)
    return pl.pallas_call(
        partial(collect_kernel, groups),
        out_shape=jax.ShapeDtypeStruct((2, groups, height, width), bf16),
        in_specs=vmem(2),
        out_specs=vmem(1)[0],
        scratch_shapes=[
            pltpu.VMEM((2, 2, groups, height, width), bf16),
            pltpu.VMEM((groups, 2, height, width), bf16),
            pltpu.VMEM((groups, 2, height, width), bf16),
            pltpu.VMEM((groups, 2, height, width), bf16),
            dma(2, groups),
            dma(2, groups),
            dma(groups),
            dma(groups),
            dma(groups),
            dma(groups),
        ],
        compiler_params=params(number),
    )(first.reshape(view), second.reshape(view))


def attention_scores(query, key, bias_row, scaling):
    length = query.shape[0]
    bias = pltpu.roll(
        jnp.broadcast_to(bias_row, (length, length)), 0, 1, stride=1, stride_axis=0
    )
    row_at = lax.broadcasted_iota(jnp.int32, (length, length), 0)
    column_at = lax.broadcasted_iota(jnp.int32, (length, length), 1)
    return jnp.where(column_at <= row_at, dot_nt(query, key) * scaling + bias, negative)


def unit_rows(rows):
    return rows * lax.rsqrt(jnp.mean(rows * rows, axis=-1, keepdims=True) + epsilon)


def forward_kernel(
    heads, size, x_ref, gain_ref, proj_ref, bias_ref, out_w_ref, qkv_ref, context_ref, log_ref, o_ref
):
    normed = (unit_rows(x_ref[...].astype(f32)) * gain_ref[...]).astype(bf16)
    for part in range(3):
        qkv_ref[part] = dot(normed, proj_ref[part]).astype(bf16)
    for head in range(heads):
        columns = slice(head * size, (head + 1) * size)
        scores = attention_scores(
            qkv_ref[0, :, columns],
            qkv_ref[1, :, columns],
            bias_ref[head : head + 1, :],
            size ** (-0.5),
        )
        peak = jnp.max(scores, axis=-1, keepdims=True)
        shifted = jnp.exp(scores - peak)
        total = jnp.sum(shifted, axis=-1, keepdims=True)
        weights = (shifted / total).astype(bf16)
        log_ref[head] = peak + jnp.log(total)
        context_ref[:, columns] = dot(weights, qkv_ref[2, :, columns]).astype(bf16)
    o_ref[...] = dot(context_ref[...], out_w_ref[...]).astype(bf16)


def backward_kernel(
    heads,
    size,
    x_ref,
    gain_ref,
    proj_ref,
    bias_ref,
    out_w_ref,
    qkv_ref,
    context_ref,
    log_ref,
    up_ref,
    grad_proj_ref,
    grad_out_ref,
    far_ref,
    wide_ref,
    first_ref,
    context_grad,
    parts,
):
    length = x_ref.shape[0]
    scaling = size ** (-0.5)
    grad_out_ref[...] = dot_tn(context_ref[...], up_ref[...])
    context_grad[...] = dot_nt(up_ref[...], out_w_ref[...]).astype(bf16)
    row_at = lax.broadcasted_iota(jnp.int32, (length, length), 0)
    column_at = lax.broadcasted_iota(jnp.int32, (length, length), 1)
    flip = (row_at + column_at == length - 1).astype(bf16)
    for head in range(heads):
        columns = slice(head * size, (head + 1) * size)
        query = qkv_ref[0, :, columns]
        key = qkv_ref[1, :, columns]
        value = qkv_ref[2, :, columns]
        pulled = context_grad[:, columns]
        scores = attention_scores(query, key, bias_ref[head : head + 1, :], scaling)
        full = jnp.exp(scores - log_ref[head])
        prob_grad = dot_nt(pulled, value)
        row_dot = jnp.sum(full * prob_grad, axis=-1, keepdims=True)
        score_grad = (full * (prob_grad - row_dot)).astype(bf16)
        parts[2, :, columns] = dot_tn(full.astype(bf16), pulled).astype(bf16)
        parts[0, :, columns] = (scaling * dot(score_grad, key)).astype(bf16)
        parts[1, :, columns] = (scaling * dot_tn(score_grad, query)).astype(bf16)
        turned = pltpu.roll(dot(flip, score_grad), 1, 1, stride=1, stride_axis=0)
        far_ref[head : head + 1, :] = jnp.sum(turned, axis=0, keepdims=True)
    unit = unit_rows(x_ref[...].astype(f32))
    normed = (unit * gain_ref[...]).astype(bf16)
    wide = jnp.zeros((length, x_ref.shape[1]), f32)
    for part in range(3):
        grad_proj_ref[part] = dot_tn(normed, parts[part])
        wide = wide + dot_nt(parts[part], proj_ref[part])
    first_ref[...] = jnp.sum(wide * unit, axis=0, keepdims=True)
    wide_ref[...] = wide.astype(bf16)


def normalize(values, scale_gain):
    return (
        values * lax.rsqrt(jnp.mean(values * values, axis=-1, keepdims=True) + epsilon) * scale_gain
    )


def per_device(
    inputs,
    projection,
    output_weight,
    first_gain,
    second_gain,
    bias_table,
    bucket_map,
    router_weight,
    routing,
    expert_up,
    expert_down,
    cotangent,
):
    local_rows, model = inputs.shape
    experts = router_weight.shape[1]
    route_count = routing.shape[1]
    capacity = max(2, 3 * route_count * local_rows // (2 * experts))
    aligned = capacity % 16 == 0
    length = local_rows * 4
    heads = bias_table.shape[0]
    width = projection.shape[2]
    size = width // heads
    slots = experts * capacity

    expert_ids = jnp.arange(experts, dtype=jnp.int32)
    route_hot = routing[:, :, None] == expert_ids[None, None, :]
    hot = jnp.sum(route_hot, axis=1).astype(bf16)
    before = jnp.tril(jnp.ones((local_rows, local_rows), bf16), -1)
    earlier = dot(before, hot)
    slot_of = jnp.sum(
        jnp.where(
            route_hot,
            earlier[:, None, :] + (expert_ids * capacity).astype(f32)[None, None, :],
            0.0,
        ),
        axis=2,
    ).astype(jnp.int32)
    slot_ids = jnp.arange(slots, dtype=jnp.int32)
    places = [
        (slot_ids[:, None] == slot_of[None, :, number]) for number in range(route_count)
    ]
    to_slots = (places[0] | places[1]).astype(bf16)
    place_hot = [place.astype(bf16) for place in places]

    reverse_map = jnp.roll(bucket_map[::-1], 1)
    reverse_hot = (
        reverse_map[None, :] == jnp.arange(bias_table.shape[1], dtype=jnp.int32)[:, None]
    ).astype(f32)
    bias_rows = jnp.dot(bias_table, reverse_hot, precision=highest)
    gain_row = first_gain[None, :]

    gathered = gather_tensor(inputs, 0)
    qkv, context, logs, attended_part = pl.pallas_call(
        partial(forward_kernel, heads, size),
        out_shape=[
            jax.ShapeDtypeStruct((3, length, width), bf16),
            jax.ShapeDtypeStruct((length, width), bf16),
            jax.ShapeDtypeStruct((heads, length, 1), f32),
            jax.ShapeDtypeStruct((length, model), bf16),
        ],
        in_specs=vmem(5),
        out_specs=vmem(4),
        compiler_params=pltpu.CompilerParams(vmem_limit_bytes=limit),
    )(gathered, gain_row, projection, bias_rows, output_weight)
    attended = scatter_tensor(attended_part, 1)

    middle = inputs.astype(f32) + attended
    second_normed = normalize(middle, second_gain).astype(bf16)
    logits = dot(second_normed, router_weight)
    chosen = jnp.sum(jnp.where(route_hot, logits[:, None, :], 0.0), axis=2)
    gate_values = jax.nn.softmax(chosen, axis=-1)
    upstream = cotangent.astype(f32)
    slot_gate = sum(
        jnp.sum(jnp.where(places[number], gate_values[None, :, number], 0.0), axis=1)
        for number in range(route_count)
    )
    send_rows = dot(to_slots, second_normed).astype(bf16)
    grad_send = (dot(to_slots, cotangent) * slot_gate[:, None]).astype(bf16)
    both = jnp.stack([send_rows, grad_send]).reshape(2, experts, capacity, model)
    if aligned:
        arrived = dispatch(both, 2).reshape(2, 4 * slots, model)
    else:
        arrived = lax.all_to_all(both, "expert", split_axis=1, concat_axis=1, tiled=True)
        arrived = lax.all_gather(arrived, "tensor", axis=1, tiled=False)
        arrived = arrived.reshape(2, 4 * slots, model)
    rows, grads = arrived[0], arrived[1]
    up, down = expert_up[0], expert_down[0]
    pre = dot(rows, up)
    act = jax.nn.gelu(pre).astype(bf16)
    out_part = dot(act, down).astype(bf16)
    act_grad = dot_nt(grads, down)
    _, gelu_pull = jax.vjp(jax.nn.gelu, pre)
    pre_grad = gelu_pull(act_grad)[0].astype(bf16)
    back_part = dot_nt(pre_grad, up).astype(bf16)
    grad_down = dot_tn(act, grads)[None]
    grad_up = dot_tn(rows, pre_grad)[None]
    if aligned:
        returned = collect(out_part, back_part, experts, 3).reshape(2, slots, model)
    else:
        returned = jnp.stack([out_part, back_part])
        returned = lax.psum_scatter(returned, "tensor", scatter_dimension=1, tiled=True)
        returned = returned.reshape(2, experts, capacity, model)
        returned = lax.all_to_all(returned, "expert", split_axis=1, concat_axis=1, tiled=True)
        returned = returned.reshape(2, slots, model)
    picked = [dot_tn(place, returned[0]) for place in place_hot]
    coming = dot_tn(to_slots, returned[1])

    result = (
        middle + gate_values[:, 0:1] * picked[0] + gate_values[:, 1:2] * picked[1]
    ).astype(bf16)
    gate_grad = jnp.stack([jnp.sum(upstream * part, axis=1) for part in picked], axis=1)
    chosen_grad = gate_values * (
        gate_grad - jnp.sum(gate_values * gate_grad, axis=1, keepdims=True)
    )
    logit_grad = jnp.sum(jnp.where(route_hot, chosen_grad[:, :, None], 0.0), axis=1)
    normed_grad = coming + jnp.dot(logit_grad, router_weight.astype(f32).T, precision=highest)
    router_part = jnp.dot(logit_grad.T, second_normed.astype(f32), precision=highest)
    _, norm_pull = jax.vjp(normalize, middle, second_gain)
    middle_back, second_part = norm_pull(normed_grad)
    middle_grad = upstream + middle_back

    rows_grad = gather_tensor(middle_grad.astype(bf16), 4)
    grad_projection, grad_output, far_sum, wide_grad, first_part = pl.pallas_call(
        partial(backward_kernel, heads, size),
        out_shape=[
            jax.ShapeDtypeStruct((3, model, width), f32),
            jax.ShapeDtypeStruct((width, model), f32),
            jax.ShapeDtypeStruct((heads, length), f32),
            jax.ShapeDtypeStruct((length, model), bf16),
            jax.ShapeDtypeStruct((1, model), f32),
        ],
        in_specs=vmem(9),
        out_specs=vmem(5),
        scratch_shapes=[
            pltpu.VMEM((length, width), bf16),
            pltpu.VMEM((3, length, width), bf16),
        ],
        compiler_params=pltpu.CompilerParams(vmem_limit_bytes=limit),
    )(gathered, gain_row, projection, bias_rows, output_weight, qkv, context, logs, rows_grad)
    table_grad = jnp.dot(far_sum, reverse_hot.T, precision=highest)
    own_grad = scatter_tensor(wide_grad, 5)
    _, first_pull = jax.vjp(normalize, inputs.astype(f32), first_gain)
    grad_inputs = middle_grad + first_pull(own_grad)[0]
    tensor_index = lax.axis_index("tensor")
    flat_table = jnp.pad(
        table_grad.reshape(1, -1), ((0, 0), (0, model // 4 - table_grad.size))
    )
    here = jnp.arange(4, dtype=jnp.int32)[:, None] == tensor_index
    table_slots = jnp.where(here, flat_table, 0.0).reshape(1, model)
    small = lax.psum(
        jnp.concatenate([first_part, second_part[None, :], table_slots, router_part], axis=0),
        ("expert", "tensor"),
    )
    own_table = jnp.sum(jnp.where(here, small[2].reshape(4, model // 4), 0.0), axis=0)
    table_grad = own_table[: table_grad.size].reshape(table_grad.shape)
    dense = lax.psum(
        (grad_projection.astype(bf16), grad_output.astype(bf16)),
        "expert",
    )
    return (
        result,
        grad_inputs,
        dense[0].astype(f32),
        dense[1].astype(f32),
        small[0],
        small[1],
        table_grad,
        small[3:].T,
        grad_up,
        grad_down,
    )


def solution(mesh):
    return jax.shard_map(
        per_device,
        mesh=mesh,
        in_specs=(
            P(("expert", "tensor"), None),
            P(None, None, "tensor"),
            P("tensor", None),
            P(),
            P(),
            P("tensor", None),
            P(),
            P(),
            P(("expert", "tensor"), None),
            P("expert", None, "tensor"),
            P("expert", "tensor", None),
            P(("expert", "tensor"), None),
        ),
        out_specs=(
            P(("expert", "tensor"), None),
            P(("expert", "tensor"), None),
            P(None, None, "tensor"),
            P("tensor", None),
            P(),
            P(),
            P("tensor", None),
            P(),
            P("expert", None, "tensor"),
            P("expert", "tensor", None),
        ),
        check_vma=False,
    )
```

time: 550 us -> 272 us (0.49); the launches traced: 543 us -> 272 us
  waiting for transfers between devices: 225 us -> 19.9 us
  Pallas kernels: 0 us -> 134 us
  local copies, waits for them, and re-layouts: 103 us -> 18.9 us
  blocking collectives: 110 us -> 42.7 us
  other arithmetic: 27.9 us -> 9.54 us
  matrix products: 49.8 us -> 31.6 us
  starting transfers between devices: 11.7 us -> 0.04 us
    pallas_call x0 -> x8, Pallas kernels: none -> 134 us  [the longest x1 45.1 us: collect(): pl.pallas_call(partial(collect_kernel, groups), out_shape=jax.ShapeDtypeS...]
    reduce_scatter x4 -> x0, waiting for transfers between devices: 80 us -> none  [the longest x1 33.2 us: per_device(): lax.psum_scatter(join_experts(pieces).astype(jnp.bfloat16), 'tensor', sca...]
    psum x2 -> x1, waiting for transfers between devices: 87.5 us -> 19.9 us  [per_device(): lax.psum((grad_projection.astype(bf16), grad_output.astype(bf16)), 'expert')]
    all_gather x2 -> x0, waiting for transfers between devices: 43.4 us -> none  [the longest x1 21.7 us: per_device(): grad_gathered = lax.all_gather(grad_arrived, 'tensor', axis=0, tiled=True)]
    all_to_all x2 -> x0, blocking collectives: 42.2 us -> none  [the longest x1 22 us: per_device(): lax.all_to_all(send_rows, 'expert', split_axis=0, concat_axis=0, tiled=True)]
    reshape x4 -> x3, local copies, waits for them, and re-layouts: 31.1 us -> 0.75 us  [the longest x1 0.66 us: per_device(): table_grad = own_table[:table_grad.size].reshape(table_grad.shape)]
    unnamed x123 -> x74, local copies, waits for them, and re-layouts: 37.4 us -> 11.2 us
    all_gather x2 -> x0, blocking collectives: 18.1 us -> none  [the longest x1 10.2 us: per_device(): gathered = lax.all_gather(inputs, 'tensor', axis=0, tiled=True)]
  transfers between devices with their start and end apart: 10 -> 1, of which waited for: 8 -> 1; matrix products, arithmetic and copies ran while one was open for 13% -> 7% of each run, Pallas kernels for 0% -> 3%
where the time goes in v1:
time: 272 us
  Pallas kernels  134 us (49%)
  blocking collectives  42.7 us (16%)
  matrix products  31.6 us (12%)
  waiting for transfers between devices  19.9 us (7%)
  local copies, waits for them, and re-layouts  18.9 us (7%)
  between operations  14.6 us (5%)
  other arithmetic  9.54 us (4%)
    pallas_call x1, Pallas kernels, collect(): pl.pallas_call(partial(collect_kernel, groups), out_shape=jax.ShapeDtypeS...  45.1 us
    psum x1, blocking collectives, per_device(): lax.psum(jnp.concatenate([first_part, second_part[None, :], table_slots,...  42.7 us
    pallas_call x1, Pallas kernels, dispatch(): pl.pallas_call(partial(dispatch_kernel, groups), out_shape=jax.ShapeDtype...  41.2 us
    psum x1, waiting for transfers between devices, per_device(): lax.psum((grad_projection.astype(bf16), grad_output.astype(bf16)), 'expert')  19.9 us
    pallas_call x2, Pallas kernels, scatter_tensor(): pl.pallas_call(scatter_kernel, out_shape=jax.ShapeDtypeStruct((height, wi...  17.5 us
    pallas_call x2, Pallas kernels, gather_tensor(): pl.pallas_call(gather_kernel, out_shape=jax.ShapeDtypeStruct((4, height,...  17.5 us
    dot_general x5, matrix products, dot_tn(): lax.dot_general(left, right, (((0,), (0,)), ((), ())), preferred_element_...  14.7 us
    unnamed x74, local copies, waits for them, and re-layouts  11.2 us
  transfers between devices with their start and end apart: 1, of which 1 were waited for; matrix products, arithmetic and copies ran while one was open for 7% of the time, Pallas kernels for 3%

profile of v1, /device:TPU:0, one launch (start us, length us, event | category | flops | bytes accessed | tf_op | source)
XLA Modules:
  0.0 271.7 jit_solution(14964288182320782789)
XLA Ops:
  7.3 0.5 multiply_convert_fusion.2
  7.8 1.2 slice.66
  9.0 0.8 slice.67
  9.9 0.7 broadcast_in_dim.122.gain_ref
  10.6 0.7 convert_reduce_fusion
  11.3 0.9 copy-done.2
  12.2 9.6 %shard_map.195 = bf16[4,128,768]{2,1,0:T(8,128)(2,1)S(1)} custom-call(bf16[128,768]{1,0:T(8,128)(2,1)S(1)} %copy-done.2), custom_call_target="tpu_custom_call" | custom-call | tf_op jit(solution)/shard_map/pallas_call | solution.py:93
  21.9 2.4 copy.29.proj_ref
  24.2 0.7 pad_add_fusion
  25.1 4.6 %shard_map.196 = (bf16[3,512,192]{2,1,0:T(8,128)(2,1)S(1)}, bf16[512,192]{1,0:T(8,128)(2,1)S(1)}, f32[3,512,1]{2,1,0:T(8,128)S(1)}, bf16[512,768]{1,0:T(8,128)(2,1)S(1)}) custom-call(bf16[512,768]{1,0:T(8,128)(2,1)S(1)} %bitcast.63, f32[1,768]{1,0:T(1,128)S(1)} %broadcast_in_dim.122.gain_ref, bf16[3,768,192]{2,1,0:T(8,128)(2,1)} %copy.29.proj_ref, ...), custom_call_target="tpu_custom_call" | custom-call | tf_op jit(solution)/shard_map/pallas_call | solution.py:451
  29.8 0.9 copy-done.5
  30.7 8.7 %shard_map.197 = f32[128,768]{1,0:T(8,128)S(1)} custom-call(bf16[2,2,128,768]{3,2,1,0:T(8,128)(2,1)S(1)} %bitcast.68), custom_call_target="tpu_custom_call" | custom-call | tf_op jit(solution)/shard_map/pallas_call | solution.py:131
  39.6 0.7 copy-done.8
  40.4 0.7 copy-done.15
  41.2 0.3 convolution_add_fusion.1
  41.6 1.2 convolution_convert_fusion.2
  42.8 0.2 select_reduce_fusion
  43.0 1.2 fusion.7
  44.4 41.2 %shard_map.198 = bf16[2,4,8,48,768]{4,3,2,1,0:T(8,128)(2,1)} custom-call(bf16[2,8,48,768]{3,2,1,0:T(8,128)(2,1)S(1)} %pad_maximum_fusion.x_ref), custom_call_target="tpu_custom_call" | custom-call | tf_op jit(solution)/shard_map/pallas_call | solution.py:203
  85.5 2.8 %fusion.52 = (bf16[1,4,8,48,768]{4,3,2,1,0:T(8,128)(2,1)S(1)}, bf16[1,4,8,48,768]{4,3,2,1,0:T(8,128)(2,1)S(1)}) fusion(bf16[2,4,8,48,768]{4,3,2,1,0:T(8,128)(2,1)} %shard_map.198), kind=kLoop, calls=%fused_computation.107 | loop fusion | bytes 9437184 | tf_op jit(solution)/shard_map/slice | solution.py:484
  88.4 2.0 fusion.14
  90.4 2.9 %convolution_convert_fusion.1 = bf16[1536,768]{1,0:T(8,128)(2,1)S(1)} fusion(bf16[1,768,768]{2,1,0:T(8,128)(2,1)S(1)} %copy-done, f32[1536,768]{1,0:T(8,128)S(1)} %fusion.14), kind=kOutput, calls=%fused_computation.11 | convolution fusion | flops 1823735808 | bytes 8257536 | tf_op jit(solution)/shard_map/dot_general | solution.py:20
  93.4 4.6 %fusion.6 = bf16[1536,768]{1,0:T(8,128)(2,1)S(1)} fusion(f32[1536,768]{1,0:T(8,128)S(1)} %fusion.14, bf16[1536,768]{1,0:T(8,128)(2,1)S(1)} %bitcast.76, bf16[1,768,768]{2,1,0:T(8,128)(2,1)S(1)} %copy-done), kind=kOutput, calls=%fused_computation.8 | convolution fusion | flops 1835532288 | bytes 10616832 | tf_op jit(solution)/shard_map/dot_general | solution.py:24
  98.0 3.5 %convolution_convert_fusion = bf16[1536,768]{1,0:T(8,128)(2,1)} fusion(bf16[1536,768]{1,0:T(8,128)(2,1)S(1)} %fusion.6, bf16[1,768,768]{2,1,0:T(8,128)(2,1)S(1)} %copy-done.31), kind=kOutput, calls=%fused_computation.10 | convolution fusion | flops 1813118976 | bytes 5898240 | tf_op jit(solution)/shard_map/dot_general | solution.py:24
  101.5 45.1 %shard_map.199 = bf16[2,8,48,768]{3,2,1,0:T(8,128)(2,1)S(1)} custom-call(bf16[2,2,8,48,768]{4,3,2,1,0:T(8,128)(2,1)S(1)} %bitcast.66, bf16[2,2,8,48,768]{4,3,2,1,0:T(8,128)(2,1)} %bitcast.78), custom_call_target="tpu_custom_call" | custom-call | tf_op jit(solution)/shard_map/pallas_call | solution.py:281
  146.8 0.3 fusion.24
  147.1 0.3 fusion.21
  147.4 0.2 copy-done.9
  147.7 1.1 fusion.16
  148.9 0.5 multiply_reduce_fusion
  149.5 0.7 copy-done.12
  150.3 7.9 %shard_map.200 = bf16[4,128,768]{2,1,0:T(8,128)(2,1)S(1)} custom-call(bf16[128,768]{1,0:T(8,128)(2,1)S(1)} %fusion.51.x_ref), custom_call_target="tpu_custom_call" | custom-call | tf_op jit(solution)/shard_map/pallas_call | solution.py:93
  158.2 0.9 copy-done.1
  159.1 8.5 %shard_map.201 = (f32[3,768,192]{2,1,0:T(8,128)}, f32[192,768]{1,0:T(8,128)S(1)}, f32[3,512]{1,0:T(4,128)S(1)}, bf16[512,768]{1,0:T(8,128)(2,1)S(1)}, f32[1,768]{1,0:T(1,128)S(1)}) custom-call(bf16[512,768]{1,0:T(8,128)(2,1)S(1)} %bitcast.64, f32[1,768]{1,0:T(1,128)S(1)} %broadcast_in_dim.122.gain_ref, bf16[3,768,192]{2,1,0:T(8,128)(2,1)} %copy.29.proj_ref, ...), custom_call_target="tpu_custom_call" | custom-call | tf_op jit(solution)/shard_map/pallas_call | solution.py:521
  167.6 0.9 copy-done.6
  168.6 0.8 convert_element_type.87
  169.3 2.8 %convert_element_type.85 = bf16[3,768,192]{2,1,0:T(8,128)(2,1)} convert(f32[3,768,192]{2,1,0:T(8,128)} %get-tuple-element.24) | non-fusion elementwise | flops 442368 | bytes 2654208 | tf_op jit(solution)/shard_map/convert_element_type | solution.py:555
  172.2 5.9 %convolution_bitcast_fusion.1 = f32[1,768,768]{2,1,0:T(8,128)} fusion(bf16[1536,768]{1,0:T(8,128)(2,1)} %bitcast.70, bf16[1536,768]{1,0:T(8,128)(2,1)} %copy-done.17), kind=kOutput, calls=%fused_computation.13 | convolution fusion | flops 1811939328 | bytes 7077888 | tf_op jit(solution)/shard_map/dot_general | solution.py:28
  178.8 42.7 %psum.23 = f32[11,768]{1,0:T(8,128)S(1)} all-reduce(f32[11,768]{1,0:T(8,128)S(1)} %pad_maximum_fusion.1), channel_id=1, replica_groups=mesh['expert'=8,'tensor'=4] {'expert','tensor'}, use_global_device_ids=true, to_apply=%region_18.19 | all-reduce | flops 8448 | bytes 67584 | tf_op jit(solution)/shard_map/psum | solution.py:548
  221.5 0.6 slice_reduce_fusion
  222.1 0.6 slice_bitcast_fusion
  222.7 8.9 %shard_map.202 = f32[128,768]{1,0:T(8,128)S(1)} custom-call(bf16[2,2,128,768]{3,2,1,0:T(8,128)(2,1)S(1)} %bitcast.67), custom_call_target="tpu_custom_call" | custom-call | tf_op jit(solution)/shard_map/pallas_call | solution.py:131
  232.0 0.7 reshape.234
  232.6 1.9 fusion.18
  234.6 7.0 %convolution_bitcast_fusion = f32[1,768,768]{2,1,0:T(8,128)} fusion(bf16[1536,768]{1,0:T(8,128)(2,1)} %bitcast.77, f32[1536,768]{1,0:T(8,128)} %copy-done.34), kind=kOutput, calls=%fused_computation.12 | convolution fusion | flops 1822556160 | bytes 9437184 | tf_op jit(solution)/shard_map/dot_general | solution.py:28
  241.6 19.9 %all-reduce.4.cloned.1.call-done = (bf16[3,768,192]{2,1,0:T(8,128)(2,1)}, bf16[192,768]{1,0:T(8,128)(2,1)}) async-done(((bf16[3,768,192]{2,1,0:T(8,128)(2,1)}, bf16[192,768]{1,0:T(8,128)(2,1)}), (bf16[3,768,192]{2,1,0:T(8,128)(2,1)}, bf16[192,768]{1,0:T(8,128)(2,1)})) %all-reduce.4.cloned.1.call-update) | async-done | bytes 1179664 | tf_op jit(solution)/shard_map/psum | solution.py:554
  261.5 2.5 copy.31
  264.0 0.9 convert_element_type.88
  (101 shorter events, 2.4 us)
Async XLA Ops:
  7.2 83.2 %copy-start = (bf16[1,768,768]{2,1,0:T(8,128)(2,1)S(1)}, bf16[1,768,768]{2,1,0:T(8,128)(2,1)}, u32[]{:S(2)}) copy-start(bf16[1,768,768]{2,1,0:T(8,128)(2,1)} %param.22) | copy-start | bytes 3538948
  7.2 17.8 %copy-start.32 = (f32[3,32]{1,0:T(4,128)S(1)}, f32[3,32]{1,0:T(4,128)}, u32[]{:S(2)}) copy-start(f32[3,32]{1,0:T(4,128)} %param.17) | copy-start | bytes 1156
  7.2 254.3 %all-reduce.4.cloned.1.call-start = ((), (), s32[]{:S(2)}) async-start(), calls=%async_computation | async-start | bytes 2949120 | tf_op jit(solution)/shard_map/psum | solution.py:554
  11.3 0.9 copy-start.2
  12.2 12.9 %copy-start.4 = (bf16[192,768]{1,0:T(8,128)(2,1)S(1)}, bf16[192,768]{1,0:T(8,128)(2,1)}, u32[]{:S(2)}) copy-start(bf16[192,768]{1,0:T(8,128)(2,1)} %out_w_ref.3) | copy-start | bytes 884740
  21.8 17.5 %copy-start.3 = (bf16[128,768]{1,0:T(8,128)(2,1)S(1)}, bf16[128,768]{1,0:T(8,128)(2,1)}, u32[]{:S(2)}) copy-start(bf16[128,768]{1,0:T(8,128)(2,1)} %x_ref.1) | copy-start | bytes 589828
  24.2 16.0 %copy-start.20 = (f32[768]{0:T(1024)S(1)}, f32[768]{0:T(1024)}, u32[]{:S(2)}) copy-start(f32[768]{0:T(1024)} %param.16) | copy-start | bytes 9220
  25.0 14.6 %copy-start.27 = (s32[512]{0:T(512)}, s32[512]{0:T(512)S(1)}, u32[]{:S(2)}) copy-start(s32[512]{0:T(512)S(1)} %pad_add_fusion) | copy-start | bytes 6148
  25.1 15.9 %copy-start.21 = (bf16[768,8]{0,1:T(8,128)(2,1)S(1)}, bf16[768,8]{0,1:T(8,128)(2,1)}, u32[]{:S(2)}) copy-start(bf16[768,8]{0,1:T(8,128)(2,1)} %param.19) | copy-start | bytes 36868
  25.1 16.1 %copy-start.33 = (f32[8]{0:T(128)S(1)}, f32[8]{0:T(128)}, u32[]{:S(2)}) copy-start(f32[8]{0:T(128)} %multiply_convert_fusion.2) | copy-start | bytes 100
  25.1 16.3 %copy-start.23 = (s32[128,2]{0,1:T(2,128)S(1)}, s32[128,2]{0,1:T(2,128)}, u32[]{:S(2)}) copy-start(s32[128,2]{0,1:T(2,128)} %param.20) | copy-start | bytes 3076
  29.8 0.9 copy-start.5
  39.5 0.7 copy-start.8
  39.5 0.8 copy-start.29
  39.5 1.6 copy-start.24
  40.4 0.7 copy-start.15
  85.5 2.8 %copy-start.31 = (bf16[1,768,768]{2,1,0:T(8,128)(2,1)S(1)}, bf16[1,768,768]{2,1,0:T(8,128)(2,1)}, u32[]{:S(2)}) copy-start(bf16[1,768,768]{2,1,0:T(8,128)(2,1)} %param.21) | copy-start | bytes 3538948
  88.3 2.1 copy-start.11
  88.3 5.0 %copy-start.18 = (bf16[1,4,8,48,768]{4,3,2,1,0:T(8,128)(2,1)}, bf16[1,4,8,48,768]{4,3,2,1,0:T(8,128)(2,1)S(1)}, u32[]{:S(2)}) copy-start(bf16[1,4,8,48,768]{4,3,2,1,0:T(8,128)(2,1)S(1)} %get-tuple-element.63) | copy-start | bytes 7077892
  90.4 3.0 %copy-start.34 = (f32[1536,768]{1,0:T(8,128)}, f32[1536,768]{1,0:T(8,128)S(1)}, u32[]{:S(2)}) copy-start(f32[1536,768]{1,0:T(8,128)S(1)} %fusion.14) | copy-start | bytes 14155780
  98.0 3.5 %copy-start.17 = (bf16[1536,768]{1,0:T(8,128)(2,1)}, bf16[1536,768]{1,0:T(8,128)(2,1)S(1)}, u32[]{:S(2)}) copy-start(bf16[1536,768]{1,0:T(8,128)(2,1)S(1)} %fusion.6) | copy-start | bytes 7077892
  146.6 1.0 copy-start.9
  146.7 1.0 copy-start.14
  146.8 2.1 copy-start.25
  146.8 2.7 copy-start.30
  149.4 0.8 copy-start.12
  158.2 0.9 copy-start.1
  167.6 0.9 copy-start.6
  172.1 6.0 %copy-start.16 = (bf16[128,768]{1,0:T(8,128)(2,1)S(1)}, bf16[128,768]{1,0:T(8,128)(2,1)}, u32[]{:S(2)}) copy-start(bf16[128,768]{1,0:T(8,128)(2,1)} %copy-done.15) | copy-start | bytes 589828
  172.2 6.2 %copy-start.28 = (s32[512]{0:T(512)S(1)}, s32[512]{0:T(512)}, u32[]{:S(2)}) copy-start(s32[512]{0:T(512)} %copy-done.27) | copy-start | bytes 6148
  172.2 50.6 %copy-start.7 = (bf16[512,768]{1,0:T(8,128)(2,1)S(1)}, bf16[512,768]{1,0:T(8,128)(2,1)}, u32[]{:S(2)}) copy-start(bf16[512,768]{1,0:T(8,128)(2,1)} %copy-done.6) | copy-start | bytes 2359300
  172.2 59.4 %copy-start.22 = (f32[768]{0:T(1024)S(1)}, f32[768]{0:T(1024)}, u32[]{:S(2)}) copy-start(f32[768]{0:T(1024)} %param.15) | copy-start | bytes 9220
  172.2 60.4 %copy-start.26 = (f32[128]{0:T(128)S(1)}, f32[128]{0:T(128)}, u32[]{:S(2)}) copy-start(f32[128]{0:T(128)} %copy-done.24) | copy-start | bytes 1540
  178.1 54.5 %copy-start.10 = (f32[128,768]{1,0:T(8,128)S(1)}, f32[128,768]{1,0:T(8,128)}, u32[]{:S(2)}) copy-start(f32[128,768]{1,0:T(8,128)} %copy-done.8) | copy-start | bytes 1179652
  178.1 54.5 %copy-start.13 = (f32[128,768]{1,0:T(8,128)S(1)}, f32[128,768]{1,0:T(8,128)}, u32[]{:S(2)}) copy-start(f32[128,768]{1,0:T(8,128)} %copy-done.12) | copy-start | bytes 1179652
  261.5 2.5 copy-start.19
Sparse Core Ops, SparseCore 0:
  172.3 89.1 all-reduce.3

commit v2 on v1

--- a/solution.py
+++ b/solution.py
@@ -299,6 +299,183 @@
     )(first.reshape(view), second.reshape(view))
 
 
+def finish_kernel(
+    groups,
+    w_ref,
+    d_ref,
+    s_ref,
+    wide_ref,
+    dense_ref,
+    small_ref,
+    got,
+    mid,
+    came,
+    halves,
+    held,
+    pieces,
+    by_tensor,
+    by_expert,
+    ws,
+    wr,
+    ts,
+    tr,
+    xs,
+    xr,
+    ys,
+    yr,
+    zs,
+    zr,
+    gs,
+    gr,
+    hs,
+    hr,
+):
+    me, core, near, far = tensor_partners()
+    side = me // 2
+    mine = lax.axis_index("expert")
+    deep = groups // 2
+    row, line = lax.rem(mine, 2), mine // 2
+    to_near, to_far = {"tensor": near}, {"tensor": far}
+    to_row = {"expert": line * 2 + 1 - row}
+    chunks = d_ref.shape[0]
+    greet(
+        [{"expert": lax.rem(mine + k, groups)} for k in range(1, groups)]
+        + [{"tensor": lax.rem(me + k, 4)} for k in range(1, 4)]
+    )
+    sends = []
+
+    def start(*arguments):
+        copy = remote(*arguments)
+        copy.start()
+        sends.append(copy)
+        return copy
+
+    for k in range(1, 4):
+        start(s_ref, by_tensor.at[me], ts.at[k], tr.at[k], {"tensor": lax.rem(me + k, 4)})
+    by_tensor[me] = s_ref[...]
+    first = [
+        start(d_ref.at[c, 1 - row], halves.at[c], ys.at[c], yr.at[c], to_row)
+        for c in range(chunks)
+    ]
+    swaps = [
+        start(
+            w_ref.at[lax.rem(side + 1 + part, 2), 1 - core],
+            got.at[part],
+            ws.at[part],
+            wr.at[part],
+            to_near,
+        )
+        for part in (0, 1)
+    ]
+    for k in range(1, 4):
+        there = lax.rem(me + 4 - k, 4)
+        remote(s_ref, by_tensor.at[there], ts.at[k], tr.at[k], {"tensor": there}).wait_recv()
+    by_expert[mine] = by_tensor[0] + by_tensor[1] + by_tensor[2] + by_tensor[3]
+    for k in range(1, groups):
+        there = lax.rem(mine + k, groups)
+        start(by_expert.at[mine], by_expert.at[mine], xs.at[k], xr.at[k], {"expert": there})
+    swaps[0].wait_recv()
+    mid[...] = (w_ref[1 - side, core].astype(f32) + got[0].astype(f32)).astype(bf16)
+    cross = start(mid, came, ws.at[2], wr.at[2], to_far)
+
+    def along(k):
+        return {"expert": lax.rem(line + k, deep) * 2 + row}
+
+    def halve(c):
+        first[c].wait_recv()
+        held[c] = (d_ref[c, row].astype(f32) + halves[c].astype(f32)).astype(bf16)
+        for k in range(1, deep):
+            start(
+                held.at[c, lax.rem(line + k, deep)],
+                pieces.at[c, k],
+                zs.at[c, k],
+                zr.at[c, k],
+                along(k),
+            )
+
+    def total(c):
+        value = held[c, line].astype(f32)
+        for k in range(1, deep):
+            remote(
+                held.at[c, line], pieces.at[c, k], zs.at[c, k], zr.at[c, k], along(k)
+            ).wait_recv()
+            value = value + pieces[c, k].astype(f32)
+        dense_ref[c, row, line] = value.astype(bf16)
+        block = dense_ref.at[c, row, line]
+        for k in range(1, deep):
+            start(block, block, gs.at[c, k], gr.at[c, k], along(k))
+
+    def spread(c):
+        for k in range(1, deep):
+            block = dense_ref.at[c, row, lax.rem(line + deep - k, deep)]
+            remote(block, block, gs.at[c, k], gr.at[c, k], along(k)).wait_recv()
+        start(dense_ref.at[c, row], dense_ref.at[c, row], hs.at[c], hr.at[c], to_row)
+
+    for step in range(chunks + 2):
+        for stage, c in ((halve, step), (total, step - 1), (spread, step - 2)):
+            if 0 <= c < chunks:
+                stage(c)
+    swaps[1].wait_recv()
+    value = w_ref[side, core].astype(f32) + got[1].astype(f32)
+    cross.wait_recv()
+    wide_ref[...] = value + came[...].astype(f32)
+    for k in range(1, groups):
+        place = lax.rem(mine + groups - k, groups)
+        block = by_expert.at[place]
+        remote(block, block, xs.at[k], xr.at[k], {"expert": place}).wait_recv()
+    value = by_expert[0]
+    for k in range(1, groups):
+        value = value + by_expert[k]
+    small_ref[...] = value
+    for c in range(chunks):
+        block = dense_ref.at[c, 1 - row]
+        remote(block, block, hs.at[c], hr.at[c], to_row).wait_recv()
+    for copy in sends:
+        copy.wait_send()
+
+
+def finish(wide, dense, small, groups, number):
+    height, width = wide.shape[0] // 4, wide.shape[1]
+    deep, chunks = groups // 2, 3
+    piece = dense.shape[0] // (chunks * groups)
+    view = (chunks, 2, deep, piece, width)
+    return pl.pallas_call(
+        partial(finish_kernel, groups),
+        out_shape=[
+            jax.ShapeDtypeStruct((height, width), f32),
+            jax.ShapeDtypeStruct(view, bf16),
+            jax.ShapeDtypeStruct(small.shape, f32),
+        ],
+        in_specs=vmem(3),
+        out_specs=vmem(3),
+        scratch_shapes=[
+            pltpu.VMEM((2, height, width), bf16),
+            pltpu.VMEM((height, width), bf16),
+            pltpu.VMEM((height, width), bf16),
+            pltpu.VMEM((chunks, deep, piece, width), bf16),
+            pltpu.VMEM((chunks, deep, piece, width), bf16),
+            pltpu.VMEM((chunks, deep, piece, width), bf16),
+            pltpu.VMEM((4,) + small.shape, f32),
+            pltpu.VMEM((groups,) + small.shape, f32),
+            dma(3),
+            dma(3),
+            dma(4),
+            dma(4),
+            dma(groups),
+            dma(groups),
+            dma(chunks),
+            dma(chunks),
+            dma(chunks, deep),
+            dma(chunks, deep),
+            dma(chunks, deep),
+            dma(chunks, deep),
+            dma(chunks),
+            dma(chunks),
+        ],
+        compiler_params=params(number),
+    )(wide.reshape(2, 2, height, width), dense.reshape(view), small)
+
+
 def attention_scores(query, key, bias_row, scaling):
     length = query.shape[0]
     bias = pltpu.roll(
@@ -318,7 +495,7 @@
 ):
     normed = (unit_rows(x_ref[...].astype(f32)) * gain_ref[...]).astype(bf16)
     for part in range(3):
-        qkv_ref[part] = dot(normed, proj_ref[part]).astype(bf16)
+        qkv_ref[part] = dot_nt(normed, proj_ref[part]).astype(bf16)
     for head in range(heads):
         columns = slice(head * size, (head + 1) * size)
         scores = attention_scores(
@@ -348,8 +525,7 @@
     context_ref,
     log_ref,
     up_ref,
-    grad_proj_ref,
-    grad_out_ref,
+    dense_ref,
     far_ref,
     wide_ref,
     first_ref,
@@ -358,7 +534,7 @@
 ):
     length = x_ref.shape[0]
     scaling = size ** (-0.5)
-    grad_out_ref[...] = dot_tn(context_ref[...], up_ref[...])
+    dense_ref[3] = dot_tn(context_ref[...], up_ref[...]).astype(bf16)
     context_grad[...] = dot_nt(up_ref[...], out_w_ref[...]).astype(bf16)
     row_at = lax.broadcasted_iota(jnp.int32, (length, length), 0)
     column_at = lax.broadcasted_iota(jnp.int32, (length, length), 1)
@@ -383,8 +559,8 @@
     normed = (unit * gain_ref[...]).astype(bf16)
     wide = jnp.zeros((length, x_ref.shape[1]), f32)
     for part in range(3):
-        grad_proj_ref[part] = dot_tn(normed, parts[part])
-        wide = wide + dot_nt(parts[part], proj_ref[part])
+        dense_ref[part] = dot_tn(parts[part], normed).astype(bf16)
+        wide = wide + dot(parts[part], proj_ref[part])
     first_ref[...] = jnp.sum(wide * unit, axis=0, keepdims=True)
     wide_ref[...] = wide.astype(bf16)
 
@@ -446,6 +622,7 @@
     ).astype(f32)
     bias_rows = jnp.dot(bias_table, reverse_hot, precision=highest)
     gain_row = first_gain[None, :]
+    turned_projection = projection.transpose(0, 2, 1)
 
     gathered = gather_tensor(inputs, 0)
     qkv, context, logs, attended_part = pl.pallas_call(
@@ -459,7 +636,7 @@
         in_specs=vmem(5),
         out_specs=vmem(4),
         compiler_params=pltpu.CompilerParams(vmem_limit_bytes=limit),
-    )(gathered, gain_row, projection, bias_rows, output_weight)
+    )(gathered, gain_row, turned_projection, bias_rows, output_weight)
     attended = scatter_tensor(attended_part, 1)
 
     middle = inputs.astype(f32) + attended
@@ -518,52 +695,60 @@
     middle_grad = upstream + middle_back
 
     rows_grad = gather_tensor(middle_grad.astype(bf16), 4)
-    grad_projection, grad_output, far_sum, wide_grad, first_part = pl.pallas_call(
+    dense_part, far_sum, wide_grad, first_part = pl.pallas_call(
         partial(backward_kernel, heads, size),
         out_shape=[
-            jax.ShapeDtypeStruct((3, model, width), f32),
-            jax.ShapeDtypeStruct((width, model), f32),
+            jax.ShapeDtypeStruct((4, width, model), bf16),
             jax.ShapeDtypeStruct((heads, length), f32),
             jax.ShapeDtypeStruct((length, model), bf16),
             jax.ShapeDtypeStruct((1, model), f32),
         ],
         in_specs=vmem(9),
-        out_specs=vmem(5),
+        out_specs=vmem(4),
         scratch_shapes=[
             pltpu.VMEM((length, width), bf16),
             pltpu.VMEM((3, length, width), bf16),
         ],
         compiler_params=pltpu.CompilerParams(vmem_limit_bytes=limit),
-    )(gathered, gain_row, projection, bias_rows, output_weight, qkv, context, logs, rows_grad)
+    )(gathered, gain_row, turned_projection, bias_rows, output_weight, qkv, context, logs, rows_grad)
     table_grad = jnp.dot(far_sum, reverse_hot.T, precision=highest)
-    own_grad = scatter_tensor(wide_grad, 5)
-    _, first_pull = jax.vjp(normalize, inputs.astype(f32), first_gain)
-    grad_inputs = middle_grad + first_pull(own_grad)[0]
     tensor_index = lax.axis_index("tensor")
     flat_table = jnp.pad(
         table_grad.reshape(1, -1), ((0, 0), (0, model // 4 - table_grad.size))
     )
     here = jnp.arange(4, dtype=jnp.int32)[:, None] == tensor_index
     table_slots = jnp.where(here, flat_table, 0.0).reshape(1, model)
-    small = lax.psum(
-        jnp.concatenate([first_part, second_part[None, :], table_slots, router_part], axis=0),
-        ("expert", "tensor"),
-    )
+    small = jnp.concatenate(
+        [
+            first_part,
+            second_part[None, :],
+            table_slots,
+            router_part,
+            jnp.zeros(((-3 - experts) % 8, model), f32),
+        ],
+        axis=0,
+    )
+    dense_rows = dense_part.reshape(4 * width, model)
+    if (4 * width) % (48 * experts) == 0:
+        own_grad, dense, small = finish(wide_grad, dense_rows, small, experts, 5)
+    else:
+        own_grad = scatter_tensor(wide_grad, 5)
+        small = lax.psum(small, ("expert", "tensor"))
+        dense = lax.psum(dense_rows, "expert")
+    dense = dense.reshape(4, width, model).astype(f32)
+    _, first_pull = jax.vjp(normalize, inputs.astype(f32), first_gain)
+    grad_inputs = middle_grad + first_pull(own_grad)[0]
     own_table = jnp.sum(jnp.where(here, small[2].reshape(4, model // 4), 0.0), axis=0)
     table_grad = own_table[: table_grad.size].reshape(table_grad.shape)
-    dense = lax.psum(
-        (grad_projection.astype(bf16), grad_output.astype(bf16)),
-        "expert",
-    )
     return (
         result,
         grad_inputs,
-        dense[0].astype(f32),
-        dense[1].astype(f32),
+        dense[:3].transpose(0, 2, 1),
+        dense[3],
         small[0],
         small[1],
         table_grad,
-        small[3:].T,
+        small[3 : 3 + experts].T,
         grad_up,
         grad_down,
     )

time: 272 us -> 228 us (0.84)
  blocking collectives: 42.7 us -> 0 us
  Pallas kernels: 134 us -> 176 us
  waiting for transfers between devices: 19.9 us -> 0 us
  between operations: 14.6 us -> 1.02 us
  matrix products: 31.6 us -> 25.8 us
  other arithmetic: 9.54 us -> 4.97 us
    pallas_call x0 -> x1, Pallas kernels: none -> 50.6 us  [finish(): pl.pallas_call(partial(finish_kernel, groups), out_shape=[jax.ShapeDtypeS...]
    psum x1 -> x0, blocking collectives: 42.7 us -> none  [per_device(): lax.psum(jnp.concatenate([first_part, second_part[None, :], table_slots,...]
    psum x1 -> x0, waiting for transfers between devices: 19.9 us -> none  [per_device(): lax.psum((grad_projection.astype(bf16), grad_output.astype(bf16)), 'expert')]
    pallas_call x2 -> x1, Pallas kernels: 17.5 us -> 8.69 us  [scatter_tensor(): pl.pallas_call(scatter_kernel, out_shape=jax.ShapeDtypeStruct((height, wi...]
    dot_general x5, matrix products: 14.7 us -> 9.22 us  [dot_tn(): lax.dot_general(left, right, (((0,), (0,)), ((), ())), preferred_element_...]
    convert_element_type x3 -> x1, other arithmetic: 4.4 us -> 0.19 us  [per_device(): dense = dense.reshape(4, width, model).astype(f32)]
    unnamed x74 -> x46, local copies, waits for them, and re-layouts: 11.2 us -> 9.49 us
  transfers between devices with their start and end apart: 1 -> 0, of which waited for: 1 -> 0; matrix products, arithmetic and copies ran while one was open for 7% -> 0% of each run, Pallas kernels for 3% -> 0%
where the time goes in v2:
time: 228 us; the launch traced here: 227 us
  Pallas kernels  176 us (77%)
  matrix products  25.8 us (11%)
  local copies, waits for them, and re-layouts  19.7 us (9%)
  other arithmetic  4.97 us (2%)
    pallas_call x1, Pallas kernels, finish(): pl.pallas_call(partial(finish_kernel, groups), out_shape=[jax.ShapeDtypeS...  50.6 us
    pallas_call x1, Pallas kernels, collect(): pl.pallas_call(partial(collect_kernel, groups), out_shape=jax.ShapeDtypeS...  45.2 us
    pallas_call x1, Pallas kernels, dispatch(): pl.pallas_call(partial(dispatch_kernel, groups), out_shape=jax.ShapeDtype...  41.2 us
    pallas_call x2, Pallas kernels, gather_tensor(): pl.pallas_call(gather_kernel, out_shape=jax.ShapeDtypeStruct((4, height,...  17.5 us
    unnamed x46, local copies, waits for them, and re-layouts  9.49 us
    dot_general x5, matrix products, dot_tn(): lax.dot_general(left, right, (((0,), (0,)), ((), ())), preferred_element_...  9.22 us
    pallas_call x1, Pallas kernels, scatter_tensor(): pl.pallas_call(scatter_kernel, out_shape=jax.ShapeDtypeStruct((height, wi...  8.69 us
    dot_general x2, matrix products, dot_nt(): lax.dot_general(left, right, (((1,), (1,)), ((), ())), preferred_element_...  8.04 us

profile of v2, /device:TPU:0, one launch (start us, length us, event | category | flops | bytes accessed | tf_op | source)
XLA Modules:
  0.0 227.2 jit_solution(4802597940730897125)
XLA Ops:
  0.7 1.3 slice.72
  2.0 0.8 slice.73
  2.9 0.7 pad_add_fusion
  3.6 0.7 broadcast_in_dim.125.gain_ref
  4.3 0.7 convert_reduce_fusion
  5.0 0.2 convolution_add_fusion.1
  5.2 0.8 convolution_bitcast_fusion.2.bias_ref
  6.0 0.9 copy-done.2
  7.0 9.6 %shard_map.195 = bf16[4,128,768]{2,1,0:T(8,128)(2,1)S(1)} custom-call(bf16[128,768]{1,0:T(8,128)(2,1)S(1)} %copy-done.2), custom_call_target="tpu_custom_call" | custom-call | tf_op jit(solution)/shard_map/pallas_call | solution.py:93
  16.6 1.0 copy-done.4
  17.6 4.6 %shard_map.196 = (bf16[3,512,192]{2,1,0:T(8,128)(2,1)S(1)}, bf16[512,192]{1,0:T(8,128)(2,1)S(1)}, f32[3,512,1]{2,1,0:T(8,128)S(1)}, bf16[512,768]{1,0:T(8,128)(2,1)S(1)}) custom-call(bf16[512,768]{1,0:T(8,128)(2,1)S(1)} %bitcast.71, f32[1,768]{1,0:T(1,128)S(1)} %broadcast_in_dim.125.gain_ref, bf16[3,192,768]{2,1,0:T(8,128)(2,1)} %bitcast.83, ...), custom_call_target="tpu_custom_call" | custom-call | tf_op jit(solution)/shard_map/pallas_call | solution.py:628
  22.2 0.9 copy-done.7
  23.0 8.7 %shard_map.197 = f32[128,768]{1,0:T(8,128)S(1)} custom-call(bf16[2,2,128,768]{3,2,1,0:T(8,128)(2,1)S(1)} %bitcast.77), custom_call_target="tpu_custom_call" | custom-call | tf_op jit(solution)/shard_map/pallas_call | solution.py:131
  31.9 0.7 copy-done.11
  32.8 0.7 copy-done.15
  33.7 0.2 select_reduce_fusion
  33.9 0.3 fusion.7
  34.2 1.2 convolution_convert_fusion.2
  35.6 41.2 %shard_map.198 = bf16[2,4,8,48,768]{4,3,2,1,0:T(8,128)(2,1)} custom-call(bf16[2,8,48,768]{3,2,1,0:T(8,128)(2,1)S(1)} %pad_maximum_fusion.x_ref), custom_call_target="tpu_custom_call" | custom-call | tf_op jit(solution)/shard_map/pallas_call | solution.py:203
  76.8 2.9 %fusion.52 = (bf16[1,4,8,48,768]{4,3,2,1,0:T(8,128)(2,1)S(1)}, bf16[1,4,8,48,768]{4,3,2,1,0:T(8,128)(2,1)S(1)}) fusion(bf16[2,4,8,48,768]{4,3,2,1,0:T(8,128)(2,1)} %shard_map.198), kind=kLoop, calls=%fused_computation.108 | loop fusion | bytes 9437184 | tf_op jit(solution)/shard_map/slice | solution.py:661
  79.7 2.0 fusion.14
  81.8 4.6 %fusion.6 = bf16[1536,768]{1,0:T(8,128)(2,1)S(1)} fusion(f32[1536,768]{1,0:T(8,128)S(1)} %fusion.14, bf16[1536,768]{1,0:T(8,128)(2,1)S(1)} %bitcast.88, bf16[1,768,768]{2,1,0:T(8,128)(2,1)S(1)} %copy-done), kind=kOutput, calls=%fused_computation.8 | convolution fusion | flops 1835532288 | bytes 10616832 | tf_op jit(solution)/shard_map/dot_general | solution.py:24
  86.4 4.0 %convolution_bitcast_fusion = f32[1,768,768]{2,1,0:T(8,128)} fusion(bf16[1536,768]{1,0:T(8,128)(2,1)S(1)} %bitcast.89, f32[1536,768]{1,0:T(8,128)S(1)} %fusion.14), kind=kOutput, calls=%fused_computation.13 | convolution fusion | flops 1822556160 | bytes 9437184 | tf_op jit(solution)/shard_map/dot_general | solution.py:28
  90.3 3.0 %convolution_convert_fusion.1 = bf16[1536,768]{1,0:T(8,128)(2,1)S(1)} fusion(bf16[1,768,768]{2,1,0:T(8,128)(2,1)S(1)} %copy-done, f32[1536,768]{1,0:T(8,128)S(1)} %fusion.14), kind=kOutput, calls=%fused_computation.11 | convolution fusion | flops 1823735808 | bytes 8257536 | tf_op jit(solution)/shard_map/dot_general | solution.py:20
  93.3 3.5 %convolution_bitcast_fusion.1 = f32[1,768,768]{2,1,0:T(8,128)} fusion(bf16[1536,768]{1,0:T(8,128)(2,1)S(1)} %bitcast.80, bf16[1536,768]{1,0:T(8,128)(2,1)S(1)} %fusion.6), kind=kOutput, calls=%fused_computation.14 | convolution fusion | flops 1811939328 | bytes 7077888 | tf_op jit(solution)/shard_map/dot_general | solution.py:28
  96.8 3.5 %convolution_convert_fusion = bf16[1536,768]{1,0:T(8,128)(2,1)} fusion(bf16[1536,768]{1,0:T(8,128)(2,1)S(1)} %fusion.6, bf16[1,768,768]{2,1,0:T(8,128)(2,1)S(1)} %copy-done.21), kind=kOutput, calls=%fused_computation.10 | convolution fusion | flops 1813118976 | bytes 5898240 | tf_op jit(solution)/shard_map/dot_general | solution.py:24
  100.3 45.2 %shard_map.199 = bf16[2,8,48,768]{3,2,1,0:T(8,128)(2,1)S(1)} custom-call(bf16[2,2,8,48,768]{4,3,2,1,0:T(8,128)(2,1)S(1)} %bitcast.74, bf16[2,2,8,48,768]{4,3,2,1,0:T(8,128)(2,1)} %bitcast.90), custom_call_target="tpu_custom_call" | custom-call | tf_op jit(solution)/shard_map/pallas_call | solution.py:281
  145.6 0.3 fusion.24
  145.9 0.3 fusion.21
  146.2 0.2 copy-done.12
  146.4 1.1 fusion.16
  147.6 0.2 fusion.55
  147.8 0.5 multiply_reduce_fusion
  148.4 0.7 copy-done.13
  149.3 7.9 %shard_map.200 = bf16[4,128,768]{2,1,0:T(8,128)(2,1)S(1)} custom-call(bf16[128,768]{1,0:T(8,128)(2,1)S(1)} %fusion.51.x_ref), custom_call_target="tpu_custom_call" | custom-call | tf_op jit(solution)/shard_map/pallas_call | solution.py:93
  157.2 0.9 copy-done.1
  158.0 8.0 %shard_map.201 = (bf16[4,192,768]{2,1,0:T(8,128)(2,1)}, f32[3,512]{1,0:T(4,128)S(1)}, bf16[512,768]{1,0:T(8,128)(2,1)S(1)}, f32[1,768]{1,0:T(1,128)S(1)}) custom-call(bf16[512,768]{1,0:T(8,128)(2,1)S(1)} %bitcast.72, f32[1,768]{1,0:T(1,128)S(1)} %broadcast_in_dim.125.gain_ref, bf16[3,192,768]{2,1,0:T(8,128)(2,1)} %bitcast.84, ...), custom_call_target="tpu_custom_call" | custom-call | tf_op jit(solution)/shard_map/pallas_call | solution.py:698
  166.0 0.9 copy-done.9
  167.5 1.3 copy-done.6
  168.7 1.1 copy-done.10
  169.9 50.6 %shard_map.202 = (f32[128,768]{1,0:T(8,128)S(1)}, bf16[3,2,4,32,768]{4,3,2,1,0:T(8,128)(2,1)S(1)}, f32[16,768]{1,0:T(8,128)S(1)}) custom-call(bf16[2,2,128,768]{3,2,1,0:T(8,128)(2,1)S(1)} %bitcast.78, bf16[3,2,4,32,768]{4,3,2,1,0:T(8,128)(2,1)S(1)} %bitcast.76, f32[16,768]{1,0:T(8,128)S(1)} %concatenate.13.s_ref), custom_call_target="tpu_custom_call" | custom-call | tf_op jit(solution)/shard_map/pallas_call | solution.py:442
  220.6 2.1 fusion.18
  222.7 0.6 slice_reduce_fusion
  223.3 0.6 slice_bitcast_fusion.2
  224.1 0.7 reshape.237
  224.8 0.2 convert.1
  225.0 0.9 slice_bitcast_fusion.1
  225.8 1.3 slice_bitcast_fusion
  (70 shorter events, 2.1 us)
Async XLA Ops:
  0.6 81.1 %copy-start = (bf16[1,768,768]{2,1,0:T(8,128)(2,1)S(1)}, bf16[1,768,768]{2,1,0:T(8,128)(2,1)}, u32[]{:S(2)}) copy-start(bf16[1,768,768]{2,1,0:T(8,128)(2,1)} %param.22) | copy-start | bytes 3538948
  6.0 0.9 copy-start.2
  7.0 24.8 %copy-start.3 = (bf16[128,768]{1,0:T(8,128)(2,1)S(1)}, bf16[128,768]{1,0:T(8,128)(2,1)}, u32[]{:S(2)}) copy-start(bf16[128,768]{1,0:T(8,128)(2,1)} %x_ref.1) | copy-start | bytes 589828
  7.0 25.7 %copy-start.17 = (f32[768]{0:T(1024)S(1)}, f32[768]{0:T(1024)}, u32[]{:S(2)}) copy-start(f32[768]{0:T(1024)} %param.16) | copy-start | bytes 9220
  16.6 1.0 copy-start.4
  17.6 15.8 %copy-start.18 = (bf16[768,8]{0,1:T(8,128)(2,1)S(1)}, bf16[768,8]{0,1:T(8,128)(2,1)}, u32[]{:S(2)}) copy-start(bf16[768,8]{0,1:T(8,128)(2,1)} %param.19) | copy-start | bytes 36868
  17.6 16.0 %copy-start.20 = (s32[128,2]{0,1:T(2,128)S(1)}, s32[128,2]{0,1:T(2,128)}, u32[]{:S(2)}) copy-start(s32[128,2]{0,1:T(2,128)} %param.20) | copy-start | bytes 3076
  17.6 16.3 %copy-start.14 = (bf16[128,768]{1,0:T(8,128)(2,1)S(1)}, bf16[128,768]{1,0:T(8,128)(2,1)}, u32[]{:S(2)}) copy-start(bf16[128,768]{1,0:T(8,128)(2,1)} %param.23) | copy-start | bytes 589828
  22.2 0.9 copy-start.7
  31.9 0.7 copy-start.11
  32.7 0.7 copy-start.15
  76.8 3.0 %copy-start.21 = (bf16[1,768,768]{2,1,0:T(8,128)(2,1)S(1)}, bf16[1,768,768]{2,1,0:T(8,128)(2,1)}, u32[]{:S(2)}) copy-start(bf16[1,768,768]{2,1,0:T(8,128)(2,1)} %param.21) | copy-start | bytes 3538948
  145.4 1.0 copy-start.12
  145.5 2.1 copy-start.16
  146.4 11.6 %copy-start.5 = (bf16[192,768]{1,0:T(8,128)(2,1)S(1)}, bf16[192,768]{1,0:T(8,128)(2,1)}, u32[]{:S(2)}) copy-start(bf16[192,768]{1,0:T(8,128)(2,1)} %out_w_ref.3) | copy-start | bytes 884740
  146.4 11.6 %copy-start.8 = (f32[3,512,1]{2,1,0:T(8,128)S(1)}, f32[3,512,1]{2,1,0:T(8,128)}, u32[]{:S(2)}) copy-start(f32[3,512,1]{2,1,0:T(8,128)} %copy-done.7) | copy-start | bytes 18436
  148.4 0.8 copy-start.13
  157.2 0.9 copy-start.1
  158.0 62.4 %copy-start.19 = (f32[768]{0:T(1024)S(1)}, f32[768]{0:T(1024)}, u32[]{:S(2)}) copy-start(f32[768]{0:T(1024)} %param.15) | copy-start | bytes 9220
  166.0 0.9 copy-start.9
  167.4 1.3 copy-start.6
  168.7 1.1 copy-start.10

commit v3 on v2

--- a/solution.py
+++ b/solution.py
@@ -66,17 +66,59 @@
     return me, core, me + 1 - 2 * core, lax.rem(me + 2, 4)
 
 
-def gather_kernel(x_ref, o_ref, send, recv, local):
+def exchange_places(ks, groups):
+    mine = lax.axis_index("expert")
+    return [{"expert": lax.rem(mine + k, groups)} for k in ks if k] + [
+        {"expert": lax.rem(mine + groups - k, groups)} for k in ks if k
+    ]
+
+
+def exchange_start(ks, groups, c_ref, co_ref, es, er, el):
+    mine = lax.axis_index("expert")
+    copies = []
+    for k in ks:
+        there = lax.rem(mine + k, groups)
+        if k:
+            copy = remote(
+                c_ref.at[there], co_ref.at[mine], es.at[k], er.at[k], {"expert": there}
+            )
+        else:
+            copy = pltpu.make_async_copy(c_ref.at[mine], co_ref.at[mine], el)
+        copy.start()
+        copies.append(copy)
+    return copies
+
+
+def exchange_wait(ks, groups, copies, c_ref, co_ref, es, er):
+    mine = lax.axis_index("expert")
+    for k, copy in zip(ks, copies):
+        if k:
+            place = lax.rem(mine + groups - k, groups)
+            remote(
+                c_ref.at[place], co_ref.at[place], es.at[k], er.at[k], {"expert": place}
+            ).wait_recv()
+            copy.wait_send()
+        else:
+            copy.wait()
+
+
+def gather_kernel(ks, groups, *refs):
+    if ks:
+        x_ref, c_ref, o_ref, co_ref, send, recv, local, es, er, el = refs
+    else:
+        x_ref, o_ref, send, recv, local = refs
     me, core, near, far = tensor_partners()
     corner = lax.rem(near + 2, 4)
     to_near, to_far = {"tensor": near}, {"tensor": far}
-    greet([to_near, to_far])
+    greet([to_near, to_far] + exchange_places(ks, groups))
     copy_far = remote(x_ref, o_ref.at[me], send.at[1], recv.at[1], to_far)
     copy_far.start()
     copy_near = remote(x_ref, o_ref.at[me], send.at[0], recv.at[0], to_near)
     copy_near.start()
     own = pltpu.make_async_copy(x_ref, o_ref.at[me], local)
     own.start()
+    if ks:
+        copies = exchange_start(ks, groups, c_ref, co_ref, es, er, el)
     remote(x_ref, o_ref.at[far], send.at[1], recv.at[1], to_far).wait_recv()
     relay = remote(o_ref.at[far], o_ref.at[far], send.at[2], recv.at[2], to_near)
     relay.start()
@@ -86,25 +128,39 @@
     copy_far.wait_send()
     copy_near.wait_send()
     relay.wait_send()
-
-
-def gather_tensor(rows, number):
+    if ks:
+        exchange_wait(ks, groups, copies, c_ref, co_ref, es, er)
+
+
+def extra_sems(ks, groups):
+    return [dma(groups), dma(groups), pltpu.SemaphoreType.DMA] if ks else []
+
+
+def gather_tensor(rows, number, ks=(), extra=()):
     height, width = rows.shape
-    return pl.pallas_call(
-        gather_kernel,
-        out_shape=jax.ShapeDtypeStruct((4, height, width), rows.dtype),
-        in_specs=vmem(1),
-        out_specs=vmem(1)[0],
-        scratch_shapes=[dma(3), dma(3), pltpu.SemaphoreType.DMA],
+    groups = extra[0].shape[0] if ks else 1
+    spaces = [pl.BlockSpec(memory_space=pl.ANY)] * len(extra)
+    outs = pl.pallas_call(
+        partial(gather_kernel, ks, groups),
+        out_shape=[jax.ShapeDtypeStruct((4, height, width), rows.dtype)]
+        + [jax.ShapeDtypeStruct(one.shape, one.dtype) for one in extra],
+        in_specs=vmem(1) + spaces,
+        out_specs=vmem(1) + spaces,
+        scratch_shapes=[dma(3), dma(3), pltpu.SemaphoreType.DMA] + extra_sems(ks, groups),
         compiler_params=params(number),
-    )(rows).reshape(4 * height, width)
-
-
-def scatter_kernel(x_ref, o_ref, got, mid, came, send, recv):
+    )(rows, *extra)
+    return [outs[0].reshape(4 * height, width)] + list(outs[1:])
+
+
+def scatter_kernel(ks, groups, *refs):
+    if ks:
+        x_ref, c_ref, o_ref, co_ref, got, mid, came, send, recv, es, er, el = refs
+    else:
+        x_ref, o_ref, got, mid, came, send, recv = refs
     me, core, near, far = tensor_partners()
     side = me // 2
     to_near, to_far = {"tensor": near}, {"tensor": far}
-    greet([to_near, to_far])
+    greet([to_near, to_far] + exchange_places(ks, groups))
     swaps = []
     for part in (0, 1):
         at_x = lax.rem(side + 1 + part, 2)
@@ -113,6 +169,8 @@
         )
         swap.start()
         swaps.append(swap)
+    if ks:
+        copies = exchange_start(ks, groups, c_ref, co_ref, es, er, el)
     swaps[0].wait_recv()
     mid[...] = (x_ref[1 - side, core].astype(f32) + got[0].astype(f32)).astype(mid.dtype)
     cross = remote(mid, came, send.at[2], recv.at[2], to_far)
@@ -124,90 +182,121 @@
     swaps[0].wait_send()
     swaps[1].wait_send()
     cross.wait_send()
-
-
-def scatter_tensor(rows, number):
+    if ks:
+        exchange_wait(ks, groups, copies, c_ref, co_ref, es, er)
+
+
+def scatter_tensor(rows, number, ks=(), extra=()):
     height, width = rows.shape[0] // 4, rows.shape[1]
+    groups = extra[0].shape[0] if ks else 1
+    spaces = [pl.BlockSpec(memory_space=pl.ANY)] * len(extra)
     return pl.pallas_call(
-        scatter_kernel,
-        out_shape=jax.ShapeDtypeStruct((height, width), f32),
-        in_specs=vmem(1),
-        out_specs=vmem(1)[0],
+        partial(scatter_kernel, ks, groups),
+        out_shape=[jax.ShapeDtypeStruct((height, width), f32)]
+        + [jax.ShapeDtypeStruct(one.shape, one.dtype) for one in extra],
+        in_specs=vmem(1) + spaces,
+        out_specs=vmem(1) + spaces,
         scratch_shapes=[
             pltpu.VMEM((2, height, width), rows.dtype),
             pltpu.VMEM((height, width), rows.dtype),
             pltpu.VMEM((height, width), rows.dtype),
             dma(3),
             dma(3),
-        ],
+        ]
+        + extra_sems(ks, groups),
         compiler_params=params(number),
-    )(rows.reshape(2, 2, height, width))
-
-
-def dispatch_kernel(groups, x_ref, o_ref, es, er, bs, br, ns, nr, cs, cr, local):
+    )(rows.reshape(2, 2, height, width), *extra)
+
+
+def dispatch_kernel(
+    groups, split, x_ref, g_ref, c1_ref, c2_ref, o_ref, go_ref, q_ref, es, er, bs, br, ns, nr, cs, cr, ls
+):
     me, core, near, far = tensor_partners()
     corner = lax.rem(near + 2, 4)
     mine = lax.axis_index("expert")
     to_near, to_far = {"tensor": near}, {"tensor": far}
     greet([{"expert": lax.rem(mine + k, groups)} for k in range(1, groups)] + [to_near, to_far])
-    own = pltpu.make_async_copy(x_ref.at[:, mine], o_ref.at[:, me, mine], local)
-    own.start()
-    sends = []
-    for k in range(1, groups):
-        there = lax.rem(mine + k, groups)
-        copy = remote(
-            x_ref.at[:, there], o_ref.at[:, me, mine], es.at[k], er.at[k], {"expert": there}
-        )
+    targets = (o_ref, go_ref, q_ref)
+    sends, locals_ = [], {}
+
+    def start(*arguments):
+        copy = remote(*arguments)
         copy.start()
         sends.append(copy)
 
     def source(k):
         return lax.rem(mine + groups - k, groups)
 
-    def relay(k):
-        place = source(k)
-        block = o_ref.at[:, far, place]
-        remote(block, block, bs.at[k], br.at[k], to_far).wait_recv()
-        copy = remote(block, block, cs.at[k], cr.at[k], to_near)
-        copy.start()
-        sends.append(copy)
-
+    for kind, ref in ((0, x_ref), (1, g_ref)):
+        own = pltpu.make_async_copy(ref.at[mine], targets[kind].at[me, mine], ls.at[kind, 0])
+        own.start()
+        locals_[kind, 0] = own
+        for k in range(1, groups):
+            there = lax.rem(mine + k, groups)
+            start(
+                ref.at[there],
+                targets[kind].at[me, mine],
+                es.at[kind, k],
+                er.at[kind, k],
+                {"expert": there},
+            )
     for k in range(groups):
         place = source(k)
-        block = o_ref.at[:, me, place]
-        if k == 0:
-            own.wait()
-        else:
-            remote(x_ref.at[:, place], block, es.at[k], er.at[k], {"expert": place}).wait_recv()
-        copy = remote(block, block, bs.at[k], br.at[k], to_far)
-        copy.start()
-        sends.append(copy)
-        copy = remote(block, block, ns.at[k], nr.at[k], to_near)
-        copy.start()
-        sends.append(copy)
-        if k > 0:
-            relay(k - 1)
-    relay(groups - 1)
+        held = (c1_ref if k < split else c2_ref).at[place]
+        block = q_ref.at[me, place]
+        start(held, block, bs.at[2, k], br.at[2, k], to_far)
+        start(held, block, ns.at[2, k], nr.at[2, k], to_near)
+        own = pltpu.make_async_copy(held, block, ls.at[2, k])
+        own.start()
+        locals_[2, k] = own
+
+    def relay(kind, k):
+        block = targets[kind].at[far, source(k)]
+        remote(block, block, bs.at[kind, k], br.at[kind, k], to_far).wait_recv()
+        start(block, block, cs.at[kind, k], cr.at[kind, k], to_near)
+
     for k in range(groups):
         place = source(k)
-        block = o_ref.at[:, near, place]
-        remote(block, block, ns.at[k], nr.at[k], to_near).wait_recv()
-        block = o_ref.at[:, corner, place]
-        remote(block, block, cs.at[k], cr.at[k], to_near).wait_recv()
+        for kind, ref in ((0, x_ref), (1, g_ref)):
+            block = targets[kind].at[me, place]
+            if k == 0:
+                locals_[kind, 0].wait()
+            else:
+                remote(
+                    ref.at[place], block, es.at[kind, k], er.at[kind, k], {"expert": place}
+                ).wait_recv()
+            start(block, block, bs.at[kind, k], br.at[kind, k], to_far)
+            start(block, block, ns.at[kind, k], nr.at[kind, k], to_near)
+        relay(2, k)
+    for k in range(groups):
+        relay(0, k)
+        relay(1, k)
+    for k in range(groups):
+        locals_[2, k].wait()
+        for kind in range(3):
+            block = targets[kind].at[near, source(k)]
+            remote(block, block, ns.at[kind, k], nr.at[kind, k], to_near).wait_recv()
+            block = targets[kind].at[corner, source(k)]
+            remote(block, block, cs.at[kind, k], cr.at[kind, k], to_near).wait_recv()
     for copy in sends:
         copy.wait_send()
 
 
-def dispatch(rows, number):
-    kinds, groups, height, width = rows.shape
+def dispatch(rows, gates, early, late, split, number):
+    groups, height, width = rows.shape
+    space = pl.BlockSpec(memory_space=pl.ANY)
     return pl.pallas_call(
-        partial(dispatch_kernel, groups),
-        out_shape=jax.ShapeDtypeStruct((kinds, 4, groups, height, width), rows.dtype),
-        in_specs=[pl.BlockSpec(memory_space=pl.ANY)],
-        out_specs=pl.BlockSpec(memory_space=pl.ANY),
-        scratch_shapes=[dma(groups)] * 8 + [pltpu.SemaphoreType.DMA],
+        partial(dispatch_kernel, groups, split),
+        out_shape=[
+            jax.ShapeDtypeStruct((4,) + rows.shape, rows.dtype),
+            jax.ShapeDtypeStruct((4,) + gates.shape, gates.dtype),
+            jax.ShapeDtypeStruct((4,) + rows.shape, rows.dtype),
+        ],
+        in_specs=[space] * 4,
+        out_specs=[space] * 3,
+        scratch_shapes=[dma(3, groups)] * 9,
         compiler_params=params(number),
-    )(rows)
+    )(rows, gates, early, late)
 
 
 def collect_kernel(groups, p_ref, g_ref, o_ref, got, mid, came, done, ps, pr, xs, xr, es, er):
@@ -624,7 +713,13 @@
     gain_row = first_gain[None, :]
     turned_projection = projection.transpose(0, 2, 1)
 
-    gathered = gather_tensor(inputs, 0)
+    spread = dot(to_slots, cotangent)
+    if aligned:
+        split = experts // 2
+        outgoing = spread.astype(bf16).reshape(experts, capacity, model)
+        gathered, early = gather_tensor(inputs, 0, tuple(range(split)), (outgoing,))
+    else:
+        gathered = gather_tensor(inputs, 0)[0]
     qkv, context, logs, attended_part = pl.pallas_call(
         partial(forward_kernel, heads, size),
         out_shape=[
@@ -637,7 +732,12 @@
         out_specs=vmem(4),
         compiler_params=pltpu.CompilerParams(vmem_limit_bytes=limit),
     )(gathered, gain_row, turned_projection, bias_rows, output_weight)
-    attended = scatter_tensor(attended_part, 1)
+    if aligned:
+        attended, late = scatter_tensor(
+            attended_part, 1, tuple(range(split, experts)), (outgoing,)
+        )
+    else:
+        attended = scatter_tensor(attended_part, 1)[0]
 
     middle = inputs.astype(f32) + attended
     second_normed = normalize(middle, second_gain).astype(bf16)
@@ -650,15 +750,23 @@
         for number in range(route_count)
     )
     send_rows = dot(to_slots, second_normed).astype(bf16)
-    grad_send = (dot(to_slots, cotangent) * slot_gate[:, None]).astype(bf16)
-    both = jnp.stack([send_rows, grad_send]).reshape(2, experts, capacity, model)
     if aligned:
-        arrived = dispatch(both, 2).reshape(2, 4 * slots, model)
+        gates = jnp.pad(
+            slot_gate.reshape(experts, 1, capacity), ((0, 0), (0, 7), (0, 128 - capacity))
+        )
+        rows, gates, grads = dispatch(
+            send_rows.reshape(experts, capacity, model), gates, early, late, split, 2
+        )
+        rows = rows.reshape(4 * slots, model)
+        gates = gates[:, :, 0, :capacity].reshape(4 * slots, 1)
+        grads = (gates * grads.reshape(4 * slots, model).astype(f32)).astype(bf16)
     else:
+        grad_send = (spread * slot_gate[:, None]).astype(bf16)
+        both = jnp.stack([send_rows, grad_send]).reshape(2, experts, capacity, model)
         arrived = lax.all_to_all(both, "expert", split_axis=1, concat_axis=1, tiled=True)
         arrived = lax.all_gather(arrived, "tensor", axis=1, tiled=False)
         arrived = arrived.reshape(2, 4 * slots, model)
-    rows, grads = arrived[0], arrived[1]
+        rows, grads = arrived[0], arrived[1]
     up, down = expert_up[0], expert_down[0]
     pre = dot(rows, up)
     act = jax.nn.gelu(pre).astype(bf16)
@@ -694,7 +802,7 @@
     middle_back, second_part = norm_pull(normed_grad)
     middle_grad = upstream + middle_back
 
-    rows_grad = gather_tensor(middle_grad.astype(bf16), 4)
+    rows_grad = gather_tensor(middle_grad.astype(bf16), 4)[0]
     dense_part, far_sum, wide_grad, first_part = pl.pallas_call(
         partial(backward_kernel, heads, size),
         out_shape=[
@@ -732,7 +840,7 @@
     if (4 * width) % (48 * experts) == 0:
         own_grad, dense, small = finish(wide_grad, dense_rows, small, experts, 5)
     else:
-        own_grad = scatter_tensor(wide_grad, 5)
+        own_grad = scatter_tensor(wide_grad, 5)[0]
         small = lax.psum(small, ("expert", "tensor"))
         dense = lax.psum(dense_rows, "expert")
     dense = dense.reshape(4, width, model).astype(f32)

time: 228 us -> 239 us (1.048)
  other arithmetic: 4.97 us -> 15.4 us
  Pallas kernels: 176 us -> 170 us
  local copies, waits for them, and re-layouts: 19.7 us -> 24 us
    pallas_call x1, Pallas kernels: 45.2 us -> 37.9 us  [collect(): pl.pallas_call(partial(collect_kernel, groups), out_shape=jax.ShapeDtypeS...]
    convert_element_type x1 -> x3, other arithmetic: 0.16 us -> 3.88 us  [the longest x2 2.72 us: per_device(): grads = (gates * grads.reshape(4 * slots, model).astype(f32)).astype(bf16)]
    unnamed x46 -> x98, local copies, waits for them, and re-layouts: 9.49 us -> 12.6 us
    slice x1, local copies, waits for them, and re-layouts: 2.93 us -> 0.05 us  [per_device(): gates = gates[:, :, 0, :capacity].reshape(4 * slots, 1)]
where the time goes in v3:
time: 239 us; the launch traced here: 238 us
  Pallas kernels  170 us (71%)
  matrix products  28 us (12%)
  local copies, waits for them, and re-layouts  24 us (10%)
  other arithmetic  15.4 us (6%)
    pallas_call x1, Pallas kernels, finish(): pl.pallas_call(partial(finish_kernel, groups), out_shape=[jax.ShapeDtypeS...  51.6 us
    pallas_call x1, Pallas kernels, collect(): pl.pallas_call(partial(collect_kernel, groups), out_shape=jax.ShapeDtypeS...  37.9 us
    pallas_call x1, Pallas kernels, dispatch(): pl.pallas_call(partial(dispatch_kernel, groups, split), out_shape=[jax.Sh...  36.4 us
    pallas_call x2, Pallas kernels, gather_tensor(): pl.pallas_call(partial(gather_kernel, ks, groups), out_shape=[jax.ShapeDt...  21.8 us
    unnamed x98, local copies, waits for them, and re-layouts  12.6 us
    pallas_call x1, Pallas kernels, scatter_tensor(): pl.pallas_call(partial(scatter_kernel, ks, groups), out_shape=[jax.ShapeD...  9.29 us
    dot_general x5, matrix products, dot_tn(): lax.dot_general(left, right, (((0,), (0,)), ((), ())), preferred_element_...  9.21 us
    dot_general x2, matrix products, dot_nt(): lax.dot_general(left, right, (((1,), (1,)), ((), ())), preferred_element_...  8.08 us

profile of v3, /device:TPU:0, one launch (start us, length us, event | category | flops | bytes accessed | tf_op | source)
XLA Modules:
  0.0 238.2 jit_solution(3346323170511987389)
XLA Ops:
  1.2 1.2 slice.69
  2.4 0.8 slice.70
  3.4 0.7 pad_add_fusion
  4.1 0.7 broadcast_in_dim.128.gain_ref
  5.6 0.7 select_reduce_fusion.4
  6.4 0.8 convolution_bitcast_fusion.2.bias_ref
  7.2 1.2 convolution_convert_fusion.3
  8.5 0.9 copy-done.2
  9.4 14.0 %shard_map.195 = (bf16[4,128,768]{2,1,0:T(8,128)(2,1)S(1)}, bf16[8,48,768]{2,1,0:T(8,128)(2,1)S(1)}) custom-call(bf16[128,768]{1,0:T(8,128)(2,1)S(1)} %copy-done.2, bf16[8,48,768]{2,1,0:T(8,128)(2,1)S(1)} %bitcast.76), custom_call_target="tpu_custom_call" | custom-call | tf_op jit(solution)/shard_map/pallas_call | solution.py:143
  23.4 1.0 copy-done.4
  24.3 4.5 %shard_map.196 = (bf16[3,512,192]{2,1,0:T(8,128)(2,1)S(1)}, bf16[512,192]{1,0:T(8,128)(2,1)S(1)}, f32[3,512,1]{2,1,0:T(8,128)S(1)}, bf16[512,768]{1,0:T(8,128)(2,1)S(1)}) custom-call(bf16[512,768]{1,0:T(8,128)(2,1)S(1)} %bitcast.78, f32[1,768]{1,0:T(1,128)S(1)} %broadcast_in_dim.128.gain_ref, bf16[3,192,768]{2,1,0:T(8,128)(2,1)} %bitcast.89, ...), custom_call_target="tpu_custom_call" | custom-call | tf_op jit(solution)/shard_map/pallas_call | solution.py:723
  28.9 0.9 copy-done.7
  30.4 9.3 %shard_map.197 = (f32[128,768]{1,0:T(8,128)S(1)}, bf16[8,48,768]{2,1,0:T(8,128)(2,1)S(1)}) custom-call(bf16[2,2,128,768]{3,2,1,0:T(8,128)(2,1)S(1)} %bitcast.86, bf16[8,48,768]{2,1,0:T(8,128)(2,1)S(1)} %bitcast.77), custom_call_target="tpu_custom_call" | custom-call | tf_op jit(solution)/shard_map/pallas_call | solution.py:193
  39.8 0.8 copy-done.11
  40.7 0.7 copy-done.15
  43.0 1.2 reduce_max.9
  44.2 0.7 fusion.46
  46.1 0.9 select_reduce_fusion
  47.6 1.4 add.90
  49.0 0.7 pad.8.g_ref
  49.7 1.2 convolution_convert_fusion.2
  50.9 1.1 copy-done.12
  52.0 36.4 %shard_map.198 = (bf16[4,8,48,768]{3,2,1,0:T(8,128)(2,1)}, f32[4,8,8,128]{3,2,1,0:T(8,128)S(1)}, bf16[4,8,48,768]{3,2,1,0:T(8,128)(2,1)}) custom-call(bf16[8,48,768]{2,1,0:T(8,128)(2,1)S(1)} %bitcast.81, f32[8,8,128]{2,1,0:T(8,128)S(1)} %pad.8.g_ref, bf16[8,48,768]{2,1,0:T(8,128)(2,1)S(1)} %get-tuple-element.31.c1_ref, bf16[8,48,768]{2,1,0:T(8,128)(2,1)S(1)} %copy-done.12), custom_call_target="tpu_custom_call" | custom-call | tf_op jit(solution)/shard_map/pallas_call | solution.py:288
  88.5 2.3 multiply_convert_fusion
  91.6 2.0 fusion.14
  93.6 4.6 %fusion.6 = bf16[1536,768]{1,0:T(8,128)(2,1)S(1)} fusion(f32[1536,768]{1,0:T(8,128)S(1)} %fusion.14, bf16[1536,768]{1,0:T(8,128)(2,1)S(1)} %bitcast.93, bf16[1,768,768]{2,1,0:T(8,128)(2,1)S(1)} %copy-done.47), kind=kOutput, calls=%fused_computation.8 | convolution fusion | flops 1835532288 | bytes 10616832 | tf_op jit(solution)/shard_map/dot_general | solution.py:24
  98.3 3.5 %convolution_bitcast_fusion.1 = f32[1,768,768]{2,1,0:T(8,128)} fusion(bf16[1536,768]{1,0:T(8,128)(2,1)S(1)} %bitcast.92, bf16[1536,768]{1,0:T(8,128)(2,1)S(1)} %fusion.6), kind=kOutput, calls=%fused_computation.17 | convolution fusion | flops 1811939328 | bytes 7077888 | tf_op jit(solution)/shard_map/dot_general | solution.py:28
  101.7 3.5 %convolution_convert_fusion = bf16[1536,768]{1,0:T(8,128)(2,1)} fusion(bf16[1536,768]{1,0:T(8,128)(2,1)S(1)} %fusion.6, bf16[1,768,768]{2,1,0:T(8,128)(2,1)S(1)} %copy-done), kind=kOutput, calls=%fused_computation.13 | convolution fusion | flops 1813118976 | bytes 5898240 | tf_op jit(solution)/shard_map/dot_general | solution.py:24
  105.2 3.9 %convolution_bitcast_fusion = f32[1,768,768]{2,1,0:T(8,128)} fusion(bf16[1536,768]{1,0:T(8,128)(2,1)S(1)} %fusion.7, f32[1536,768]{1,0:T(8,128)S(1)} %fusion.14), kind=kOutput, calls=%fused_computation.16 | convolution fusion | flops 1822556160 | bytes 9437184 | tf_op jit(solution)/shard_map/dot_general | solution.py:28
  109.2 2.9 %convolution_convert_fusion.1 = bf16[1536,768]{1,0:T(8,128)(2,1)S(1)} fusion(bf16[1,768,768]{2,1,0:T(8,128)(2,1)S(1)} %copy-done.47, f32[1536,768]{1,0:T(8,128)S(1)} %fusion.14), kind=kOutput, calls=%fused_computation.14 | convolution fusion | flops 1823735808 | bytes 8257536 | tf_op jit(solution)/shard_map/dot_general | solution.py:20
  112.2 37.9 %shard_map.199 = bf16[2,8,48,768]{3,2,1,0:T(8,128)(2,1)S(1)} custom-call(bf16[2,2,8,48,768]{4,3,2,1,0:T(8,128)(2,1)S(1)} %bitcast.82, bf16[2,2,8,48,768]{4,3,2,1,0:T(8,128)(2,1)} %bitcast.95), custom_call_target="tpu_custom_call" | custom-call | tf_op jit(solution)/shard_map/pallas_call | solution.py:370
  151.0 1.1 fusion.16
  152.3 0.8 fusion.54
  153.1 1.2 multiply_reduce_fusion
  155.4 1.2 fusion.51.refs_0_
  156.5 7.9 %shard_map.200 = bf16[4,128,768]{2,1,0:T(8,128)(2,1)S(1)} custom-call(bf16[128,768]{1,0:T(8,128)(2,1)S(1)} %fusion.51.refs_0_), custom_call_target="tpu_custom_call" | custom-call | tf_op jit(solution)/shard_map/pallas_call | solution.py:143
  164.4 0.9 copy-done.1
  165.3 8.0 %shard_map.201 = (bf16[4,192,768]{2,1,0:T(8,128)(2,1)}, f32[3,512]{1,0:T(4,128)S(1)}, bf16[512,768]{1,0:T(8,128)(2,1)S(1)}, f32[1,768]{1,0:T(1,128)S(1)}) custom-call(bf16[512,768]{1,0:T(8,128)(2,1)S(1)} %bitcast.79, f32[1,768]{1,0:T(1,128)S(1)} %broadcast_in_dim.128.gain_ref, bf16[3,192,768]{2,1,0:T(8,128)(2,1)} %bitcast.90, ...), custom_call_target="tpu_custom_call" | custom-call | tf_op jit(solution)/shard_map/pallas_call | solution.py:806
  173.3 0.9 copy-done.9
  174.4 0.7 broadcast_select_fusion
  175.2 1.6 concatenate.12.s_ref
  176.8 1.3 copy-done.6
  178.1 1.1 copy-done.10
  179.2 51.6 %shard_map.202 = (f32[128,768]{1,0:T(8,128)S(1)}, bf16[3,2,4,32,768]{4,3,2,1,0:T(8,128)(2,1)S(1)}, f32[16,768]{1,0:T(8,128)S(1)}) custom-call(bf16[2,2,128,768]{3,2,1,0:T(8,128)(2,1)S(1)} %bitcast.85, bf16[3,2,4,32,768]{4,3,2,1,0:T(8,128)(2,1)S(1)} %bitcast.84, f32[16,768]{1,0:T(8,128)S(1)} %concatenate.12.s_ref), custom_call_target="tpu_custom_call" | custom-call | tf_op jit(solution)/shard_map/pallas_call | solution.py:531
  230.8 0.8 fusion.19
  231.7 2.0 fusion.18
  236.0 0.9 slice_bitcast_fusion.1
  236.8 1.3 slice_bitcast_fusion
  (127 shorter events, 11.3 us)
Async XLA Ops:
  0.6 90.7 %copy-start = (bf16[1,768,768]{2,1,0:T(8,128)(2,1)S(1)}, bf16[1,768,768]{2,1,0:T(8,128)(2,1)}, u32[]{:S(2)}) copy-start(bf16[1,768,768]{2,1,0:T(8,128)(2,1)} %param.21) | copy-start | bytes 3538948
  0.7 40.8 %copy-start.22 = (f32[768]{0:T(1024)S(1)}, f32[768]{0:T(1024)}, u32[]{:S(2)}) copy-start(f32[768]{0:T(1024)} %param.16) | copy-start | bytes 9220
  0.7 39.9 %copy-start.3 = (bf16[128,768]{1,0:T(8,128)(2,1)S(1)}, bf16[128,768]{1,0:T(8,128)(2,1)}, u32[]{:S(2)}) copy-start(bf16[128,768]{1,0:T(8,128)(2,1)} %refs_0_.1) | copy-start | bytes 589828
  3.3 39.0 %copy-start.23 = (bf16[768,8]{0,1:T(8,128)(2,1)S(1)}, bf16[768,8]{0,1:T(8,128)(2,1)}, u32[]{:S(2)}) copy-start(bf16[768,8]{0,1:T(8,128)(2,1)} %param.19) | copy-start | bytes 36868
  3.3 39.1 %copy-start.30 = (s32[128,2]{0,1:T(2,128)S(1)}, s32[128,2]{0,1:T(2,128)}, u32[]{:S(2)}) copy-start(s32[128,2]{0,1:T(2,128)} %param.20) | copy-start | bytes 3076
  4.1 19.3 %copy-start.42 = (s32[512]{0:T(512)}, s32[512]{0:T(512)S(1)}, u32[]{:S(2)}) copy-start(s32[512]{0:T(512)S(1)} %pad_add_fusion) | copy-start | bytes 6148
  6.4 17.0 %copy-start.26 = (s32[128]{0:T(128)}, s32[128]{0:T(128)S(1)}, u32[]{:S(2)}) copy-start(s32[128]{0:T(128)S(1)} %get-tuple-element.65) | copy-start | bytes 1540
  6.4 17.0 %copy-start.28 = (s32[128]{0:T(128)}, s32[128]{0:T(128)S(1)}, u32[]{:S(2)}) copy-start(s32[128]{0:T(128)S(1)} %get-tuple-element.64) | copy-start | bytes 1540
  8.5 0.9 copy-start.2
  23.4 1.0 copy-start.4
  28.9 0.9 copy-start.7
  29.8 0.7 copy-start.13
  39.7 0.8 copy-start.11
  40.7 0.7 copy-start.15
  40.7 1.7 copy-start.45
  41.5 0.9 copy-start.35
  41.6 0.7 copy-start.19
  44.9 0.7 copy-start.33
  45.6 0.5 copy-start.37
  45.6 1.4 copy-start.39
  50.9 1.1 copy-start.12
  88.5 2.4 copy-start.17
  88.5 3.1 %copy-start.21 = (bf16[4,8,48,768]{3,2,1,0:T(8,128)(2,1)S(1)}, bf16[4,8,48,768]{3,2,1,0:T(8,128)(2,1)}, u32[]{:S(2)}) copy-start(bf16[4,8,48,768]{3,2,1,0:T(8,128)(2,1)} %get-tuple-element.33) | copy-start | bytes 7077892
  91.6 2.0 copy-start.47
  112.1 38.2 %copy-start.27 = (s32[128]{0:T(128)S(1)}, s32[128]{0:T(128)}, u32[]{:S(2)}) copy-start(s32[128]{0:T(128)} %copy-done.26) | copy-start | bytes 1540
  112.1 38.2 %copy-start.29 = (s32[128]{0:T(128)S(1)}, s32[128]{0:T(128)}, u32[]{:S(2)}) copy-start(s32[128]{0:T(128)} %copy-done.28) | copy-start | bytes 1540
  112.1 38.9 %copy-start.16 = (f32[128,768]{1,0:T(8,128)S(1)}, f32[128,768]{1,0:T(8,128)}, u32[]{:S(2)}) copy-start(f32[128,768]{1,0:T(8,128)} %copy-done.15) | copy-start | bytes 1179652
  112.1 38.9 %copy-start.18 = (bf16[128,768]{1,0:T(8,128)(2,1)S(1)}, bf16[128,768]{1,0:T(8,128)(2,1)}, u32[]{:S(2)}) copy-start(bf16[128,768]{1,0:T(8,128)(2,1)} %param.23) | copy-start | bytes 589828
  112.2 38.9 %copy-start.38 = (f32[128]{0:T(128)S(1)}, f32[128]{0:T(128)}, u32[]{:S(2)}) copy-start(f32[128]{0:T(128)} %copy-done.37) | copy-start | bytes 1540
  112.2 38.9 %copy-start.40 = (f32[128]{0:T(128)S(1)}, f32[128]{0:T(128)}, u32[]{:S(2)}) copy-start(f32[128]{0:T(128)} %copy-done.39) | copy-start | bytes 1540
  112.2 40.0 %copy-start.25 = (f32[128,2]{0,1:T(2,128)S(1)}, f32[128,2]{0,1:T(2,128)}, u32[]{:S(2)}) copy-start(f32[128,2]{0,1:T(2,128)} %select_reduce_fusion.3) | copy-start | bytes 3076
  112.2 40.0 %copy-start.32 = (f32[128]{0:T(128)S(1)}, f32[128]{0:T(128)}, u32[]{:S(2)}) copy-start(f32[128]{0:T(128)} %reduce_max.9) | copy-start | bytes 1540
  112.2 40.0 %copy-start.34 = (f32[128]{0:T(128)S(1)}, f32[128]{0:T(128)}, u32[]{:S(2)}) copy-start(f32[128]{0:T(128)} %copy-done.33) | copy-start | bytes 1540
  112.2 40.0 %copy-start.31 = (s32[128,2]{0,1:T(2,128)S(1)}, s32[128,2]{0,1:T(2,128)}, u32[]{:S(2)}) copy-start(s32[128,2]{0,1:T(2,128)} %param.20) | copy-start | bytes 3076
  112.2 40.0 %copy-start.20 = (bf16[128,768]{1,0:T(8,128)(2,1)S(1)}, bf16[128,768]{1,0:T(8,128)(2,1)}, u32[]{:S(2)}) copy-start(bf16[128,768]{1,0:T(8,128)(2,1)} %copy-done.19) | copy-start | bytes 589828
  112.2 40.8 %copy-start.24 = (bf16[768,8]{0,1:T(8,128)(2,1)S(1)}, bf16[768,8]{0,1:T(8,128)(2,1)}, u32[]{:S(2)}) copy-start(bf16[768,8]{0,1:T(8,128)(2,1)} %param.19) | copy-start | bytes 36868
  112.2 40.8 %copy-start.36 = (f32[128]{0:T(128)S(1)}, f32[128]{0:T(128)}, u32[]{:S(2)}) copy-start(f32[128]{0:T(128)} %copy-done.35) | copy-start | bytes 1540
  150.2 4.7 %copy-start.46 = (f32[128]{0:T(128)S(1)}, f32[128]{0:T(128)}, u32[]{:S(2)}) copy-start(f32[128]{0:T(128)} %copy-done.45) | copy-start | bytes 1540
  150.2 15.1 %copy-start.5 = (bf16[192,768]{1,0:T(8,128)(2,1)S(1)}, bf16[192,768]{1,0:T(8,128)(2,1)}, u32[]{:S(2)}) copy-start(bf16[192,768]{1,0:T(8,128)(2,1)} %out_w_ref.3) | copy-start | bytes 884740
  150.2 15.1 %copy-start.8 = (f32[3,512,1]{2,1,0:T(8,128)S(1)}, f32[3,512,1]{2,1,0:T(8,128)}, u32[]{:S(2)}) copy-start(f32[3,512,1]{2,1,0:T(8,128)} %copy-done.7) | copy-start | bytes 18436
  150.2 15.1 %copy-start.14 = (bf16[512,192]{1,0:T(8,128)(2,1)S(1)}, bf16[512,192]{1,0:T(8,128)(2,1)}, u32[]{:S(2)}) copy-start(bf16[512,192]{1,0:T(8,128)(2,1)} %copy-done.13) | copy-start | bytes 589828
  151.0 23.2 %copy-start.43 = (s32[512]{0:T(512)S(1)}, s32[512]{0:T(512)}, u32[]{:S(2)}) copy-start(s32[512]{0:T(512)} %copy-done.42) | copy-start | bytes 6148
  154.9 0.5 copy-start.41
  164.4 0.9 copy-start.1
  173.3 0.9 copy-start.9
  174.2 60.8 %copy-start.44 = (pred[4]{0:T(512)(128)(4,1)S(1)}, pred[4]{0:T(512)(128)(4,1)}, u32[]{:S(2)}) copy-start(pred[4]{0:T(512)(128)(4,1)} %iota_compare_fusion.9) | copy-start | bytes 16
  176.8 1.3 copy-start.6
  178.1 1.1 copy-start.10
